TPU v7x, 512 devices: a whole 4x4x16 slice. The times are simulated.
512 devices in a mesh: seq: 64 (over y, z), head: 8 (over x, core).
Axes of the slice: x: 4, y: 4, z: 16, core: 2. Of those that a mesh axis runs over, the one named last changes fastest.
Arguments:
- query_rows: bfloat16 [32768, 1024], P(('seq', 'head')), may hold values from -6 to 6
- key_rows: bfloat16 [32768, 1024], P(('seq', 'head')), may hold values from -6 to 6
- value_rows: bfloat16 [32768, 1024], P(('seq', 'head')), may hold values from -6 to 6
- out_grad: bfloat16 [32768, 1024], P(('seq', 'head')), may hold values from -6 to 6
- random_ids: int32 [512, 3], replicated, may hold values from 0 to 511, as said below
- global_ids: int32 [2], replicated, may hold values from 0 to 511, as said below
Outputs:
- attn_out: bfloat16 [32768, 1024], P(('seq', 'head'))
- query_grad: bfloat16 [32768, 1024], P(('seq', 'head'))
- key_grad: bfloat16 [32768, 1024], P(('seq', 'head'))
- value_grad: bfloat16 [32768, 1024], P(('seq', 'head'))
Inputs may be any that keep to these rules, and one draw needn't show every extreme that they name: `global_ids`: the two are different, and one of them is block 511. Group g holds query and key blocks g * 8 to g * 8 + 7. For every group, count per group (itself included) the key blocks it reads there: the block just before the group and the block just after it (each once, where present), each of the two global blocks once, and every entry of its rows of random_ids. No count exceeds 3, and for every group some count is exactly 3.
All inputs are finite; a program needn't handle non-finite values.
Results may differ from a plain program's by a relative error of at most 0.0069.
Values may be sent and summed in bfloat16 or wider, within the bound.
A program may use at most 64 MiB of HBM per device.

v0:
```python
import jax
import jax.numpy as jnp
from jax import lax
from jax.sharding import PartitionSpec as P

HD = 128
BLOCK = 64
QB_DEV = 8


def request_tables(random_ids, global_ids, group_count):
    group_index = jnp.arange(group_count, dtype=jnp.int32)
    first_block = group_index * QB_DEV
    rand_blocks = random_ids.reshape(group_count, 3 * QB_DEV)
    global_pair = jnp.broadcast_to(global_ids[None, :], (group_count, 2))
    blocks = jnp.concatenate(
        [(first_block - 1)[:, None], (first_block + QB_DEV)[:, None], global_pair, rand_blocks],
        axis=1,
    )
    usable = jnp.concatenate(
        [
            (group_index > 0)[:, None],
            (group_index < group_count - 1)[:, None],
            jnp.full((group_count, 2), True, dtype=jnp.bool_),
            jnp.ones(rand_blocks.shape, dtype=jnp.bool_),
        ],
        axis=1,
    )
    blocks = jnp.clip(blocks, 0, group_count * QB_DEV - 1)
    owners = jnp.where(usable, blocks // QB_DEV, -1)
    inner_block = blocks % QB_DEV
    entry_count = blocks.shape[1]
    matches = owners[:, :, None] == owners[:, None, :]
    earlier = jnp.arange(entry_count)[None, :] < jnp.arange(entry_count)[:, None]
    order_in_owner = jnp.sum(matches & earlier[None, :, :], axis=2)
    return (owners, inner_block, usable, order_in_owner)


def slot_tiles(local_tiles, left_tile, right_tile, global_tiles, random_tiles):
    extended = jnp.concatenate([left_tile[None], local_tiles, right_tile[None]], axis=0)
    window = jnp.stack(
        [extended[0:QB_DEV], extended[1 : QB_DEV + 1], extended[2 : QB_DEV + 2]], axis=1
    )
    global_rep = jnp.broadcast_to(global_tiles[None], (QB_DEV,) + global_tiles.shape)
    return jnp.concatenate([window, global_rep, random_tiles], axis=1)


def shards(query_rows, key_rows, value_rows, out_grad, random_ids, global_ids):
    group_count = lax.axis_size("seq")
    my_group = lax.axis_index("seq")
    capacity = max(3, (3 * QB_DEV + 4 + group_count - 1) // group_count + 1)
    score_scale = HD ** (-0.5)
    arrived = (
        lax.all_to_all(query_rows, "head", split_axis=1, concat_axis=0, tiled=True),
        lax.all_to_all(key_rows, "head", split_axis=1, concat_axis=0, tiled=True),
        lax.all_to_all(value_rows, "head", split_axis=1, concat_axis=0, tiled=True),
        lax.all_to_all(out_grad, "head", split_axis=1, concat_axis=0, tiled=True),
    )
    row_count = arrived[0].shape[0]
    heads_here = arrived[0].shape[1] // HD

    def as_tiles(rows):
        return rows.reshape(QB_DEV, BLOCK, heads_here, HD)

    query_blk = as_tiles(arrived[0])
    key_blk = as_tiles(arrived[1])
    value_blk = as_tiles(arrived[2])
    grad_blk = as_tiles(arrived[3])
    owners, inner_block, usable, order_in_owner = request_tables(
        random_ids, global_ids, group_count
    )
    slot_total = group_count * capacity
    my_owner = owners[my_group]
    my_slot = jnp.where(
        usable[my_group], my_owner * capacity + order_in_owner[my_group], slot_total
    )
    to_me = owners == my_group
    pick = to_me[:, :, None] & (
        order_in_owner[:, :, None] == jnp.arange(capacity, dtype=jnp.int32)[None, None, :]
    )
    send_inner = jnp.sum(jnp.where(pick, inner_block[:, :, None], 0), axis=1).reshape(-1)
    pair_blk = jnp.stack([key_blk, value_blk], axis=1)
    outgoing = jnp.take(pair_blk, send_inner, axis=0).reshape(
        (group_count, capacity) + pair_blk.shape[1:]
    )
    incoming = lax.all_to_all(outgoing, "seq", split_axis=0, concat_axis=0, tiled=True)
    incoming_flat = incoming.reshape((slot_total,) + pair_blk.shape[1:])
    fetched = jnp.take(incoming_flat, jnp.minimum(my_slot, slot_total - 1), axis=0)
    global_tiles = fetched[2:4]
    random_tiles = fetched[4:].reshape((QB_DEV, 3) + pair_blk.shape[1:])
    key_sel = slot_tiles(
        key_blk, fetched[0, 0], fetched[1, 0], global_tiles[:, 0], random_tiles[:, :, 0]
    )
    value_sel = slot_tiles(
        value_blk, fetched[0, 1], fetched[1, 1], global_tiles[:, 1], random_tiles[:, :, 1]
    )
    block_ids = my_group * QB_DEV + jnp.arange(QB_DEV, dtype=jnp.int32)
    slot_ok = jnp.concatenate(
        [
            (block_ids > 0)[:, None],
            jnp.ones((QB_DEV, 1), dtype=jnp.bool_),
            (block_ids < group_count * QB_DEV - 1)[:, None],
            jnp.ones((QB_DEV, 5), dtype=jnp.bool_),
        ],
        axis=1,
    )
    scores = (
        jnp.einsum("qbhd,qjkhd->qhbjk", query_blk, key_sel, preferred_element_type=jnp.float32)
        * score_scale
    )
    scores = jnp.where(slot_ok[:, None, None, :, None], scores, -jnp.inf)
    row_max = jnp.max(scores, axis=(3, 4), keepdims=True)
    expo = jnp.exp(scores - row_max)
    weights = expo / jnp.sum(expo, axis=(3, 4), keepdims=True)
    prob_bf = weights.astype(jnp.bfloat16)
    attention = jnp.einsum(
        "qhbjk,qjkhd->qbhd", prob_bf, value_sel, preferred_element_type=jnp.float32
    )
    attn_out = attention.astype(jnp.bfloat16).reshape(row_count, -1)
    row_delta = jnp.sum(grad_blk.astype(jnp.float32) * attention, axis=3)
    dprobs = jnp.einsum(
        "qbhd,qjkhd->qhbjk", grad_blk, value_sel, preferred_element_type=jnp.float32
    )
    delta_t = jnp.transpose(row_delta, (0, 2, 1))[:, :, :, None, None]
    dscores = (weights * (dprobs - delta_t)).astype(jnp.bfloat16)
    query_grad = (
        jnp.einsum("qhbjk,qjkhd->qbhd", dscores, key_sel, preferred_element_type=jnp.float32)
        * score_scale
    ).astype(jnp.bfloat16)
    win_key = (
        jnp.einsum(
            "qhbjk,qbhd->qjkhd",
            dscores[:, :, :, 0:3],
            query_blk,
            preferred_element_type=jnp.float32,
        )
        * score_scale
    )
    win_value = jnp.einsum(
        "qhbjk,qbhd->qjkhd", prob_bf[:, :, :, 0:3], grad_blk, preferred_element_type=jnp.float32
    )
    glob_key = (
        jnp.einsum(
            "qhbjk,qbhd->jkhd", dscores[:, :, :, 3:5], query_blk, preferred_element_type=jnp.float32
        )
        * score_scale
    )
    glob_value = jnp.einsum(
        "qhbjk,qbhd->jkhd", prob_bf[:, :, :, 3:5], grad_blk, preferred_element_type=jnp.float32
    )
    rand_key = (
        jnp.einsum(
            "qhbjk,qbhd->qjkhd",
            dscores[:, :, :, 5:8],
            query_blk,
            preferred_element_type=jnp.float32,
        )
        * score_scale
    )
    rand_value = jnp.einsum(
        "qhbjk,qbhd->qjkhd", prob_bf[:, :, :, 5:8], grad_blk, preferred_element_type=jnp.float32
    )
    window_terms = jnp.stack([win_key, win_value], axis=2)
    pad_rest = ((0, 0),) * 4
    extended_grad = (
        jnp.pad(window_terms[:, 0], ((0, 2),) + pad_rest)
        + jnp.pad(window_terms[:, 1], ((1, 1),) + pad_rest)
        + jnp.pad(window_terms[:, 2], ((2, 0),) + pad_rest)
    )
    local_acc = extended_grad[1 : QB_DEV + 1]
    rand_terms = jnp.stack([rand_key, rand_value], axis=2).reshape(
        (3 * QB_DEV,) + pair_blk.shape[1:]
    )
    empty_pair = jnp.zeros((2,) + pair_blk.shape[1:], jnp.float32)
    returning = jnp.concatenate(
        [extended_grad[0:1], extended_grad[QB_DEV + 1 : QB_DEV + 2], empty_pair, rand_terms], axis=0
    ).astype(jnp.bfloat16)
    send_back = (
        jnp.zeros((slot_total,) + pair_blk.shape[1:], jnp.bfloat16)
        .at[my_slot]
        .add(returning, mode="drop")
    )
    came_back = lax.all_to_all(
        send_back.reshape((group_count, capacity) + pair_blk.shape[1:]),
        "seq",
        split_axis=0,
        concat_axis=0,
        tiled=True,
    )
    local_acc = local_acc.at[send_inner].add(
        came_back.reshape((slot_total,) + pair_blk.shape[1:]).astype(jnp.float32)
    )
    glob_terms = jnp.stack([glob_key, glob_value], axis=1)
    glob_sums = lax.psum(glob_terms, "seq")
    owner_mask = (global_ids // QB_DEV == my_group).astype(jnp.float32)
    local_acc = local_acc.at[global_ids % QB_DEV].add(
        glob_sums * owner_mask[:, None, None, None, None]
    )
    query_grad = query_grad.reshape(row_count, -1)
    key_grad = local_acc[:, 0].astype(jnp.bfloat16).reshape(row_count, -1)
    value_grad = local_acc[:, 1].astype(jnp.bfloat16).reshape(row_count, -1)
    all_back = (
        lax.all_to_all(attn_out, "head", split_axis=0, concat_axis=1, tiled=True),
        lax.all_to_all(query_grad, "head", split_axis=0, concat_axis=1, tiled=True),
        lax.all_to_all(key_grad, "head", split_axis=0, concat_axis=1, tiled=True),
        lax.all_to_all(value_grad, "head", split_axis=0, concat_axis=1, tiled=True),
    )
    return (all_back[0], all_back[1], all_back[2], all_back[3])


def solution(mesh):
    return jax.shard_map(
        shards,
        mesh=mesh,
        in_specs=(
            P(("seq", "head"), None),
            P(("seq", "head"), None),
            P(("seq", "head"), None),
            P(("seq", "head"), None),
            P(),
            P(),
        ),
        out_specs=(
            P(("seq", "head"), None),
            P(("seq", "head"), None),
            P(("seq", "head"), None),
            P(("seq", "head"), None),
        ),
        check_vma=False,
    )
```

profile of v0, /device:TPU:1, one launch (start us, length us, event | category | flops | bytes accessed | tf_op | source)
XLA Modules:
  0.0 808.7 jit_solution(3880111259703941456)
XLA Ops:
  8.8 10.2 %all-to-all-start = ((bf16[64,8,128]{2,0,1:T(8,128)(2,1)}), bf16[64,8,128]{2,0,1:T(8,128)(2,1)S(1)}, u32[]{:S(2)}, u32[]{:S(2)}) async-start(bf16[64,8,128]{2,0,1:T(8,128)(2,1)} %copy_bitcast_fusion.7), calls=%async_computation | async-start | bytes 262144 | tf_op jit(solution)/shard_map/all_to_all | solution.py:55
  19.1 1.6 copy_bitcast_fusion.6
  23.2 1.0 all-to-all-done
  24.2 4.1 all-to-all-start.1
  28.5 5.2 all-to-all-done.1
  33.7 7.9 gather_fusion
  41.6 6.1 broadcast_select_fusion
  47.6 14.4 %all-to-all-start.2 = ((bf16[64,3,2,64,1,128]{5,3,2,1,4,0:T(8,128)(2,1)}), bf16[64,3,2,64,1,128]{5,3,2,1,4,0:T(8,128)(2,1)}, u32[]{:S(2)}, u32[]{:S(2)}) async-start(bf16[64,3,2,64,1,128]{5,3,2,1,4,0:T(8,128)(2,1)} %broadcast_select_fusion), calls=%async_computation.2 | async-start | bytes 12582912 | tf_op jit(solution)/shard_map/all_to_all | solution.py:86
  65.0 270.4 %all-to-all-done.2 = bf16[64,3,2,64,1,128]{5,3,2,1,4,0:T(8,128)(2,1)} async-done(((bf16[64,3,2,64,1,128]{5,3,2,1,4,0:T(8,128)(2,1)}), bf16[64,3,2,64,1,128]{5,3,2,1,4,0:T(8,128)(2,1)}, u32[]{:S(2)}, u32[]{:S(2)}) %all-to-all-start.2) | async-done | bytes 6291488 | tf_op jit(solution)/shard_map/all_to_all | solution.py:86
  335.4 9.7 %all-to-all-start.3 = ((bf16[64,8,128]{2,0,1:T(8,128)(2,1)}), bf16[64,8,128]{2,0,1:T(8,128)(2,1)S(1)}, u32[]{:S(2)}, u32[]{:S(2)}) async-start(bf16[64,8,128]{2,0,1:T(8,128)(2,1)} %copy_bitcast_fusion.5), calls=%async_computation.3 | async-start | bytes 262144 | tf_op jit(solution)/shard_map/all_to_all | solution.py:54
  345.1 3.5 gather_fusion.1
  352.9 4.8 all-to-all-start.5
  358.8 1.5 convert_bitcast_fusion
  360.3 2.7 all-to-all-done.5
  363.0 2.7 fusion.24
  365.7 2.0 fusion
  368.8 1.1 fusion.8
  369.9 4.1 all-to-all-start.6
  374.1 1.2 fusion.4
  375.9 1.2 fusion.5
  377.6 4.2 broadcast.559
  381.8 6.4 scatter_fusion
  388.2 6.5 all-to-all-start.7
  395.0 1.2 fusion.10
  397.7 331.9 %all-reduce.5.cloned.1.call-done = f32[2,2,64,1,128]{4,2,0,3,1:T(8,128)} async-done(((f32[2,2,64,1,128]{4,2,0,3,1:T(8,128)}), f32[2,2,64,1,128]{4,2,0,3,1:T(8,128)}) %all-reduce.5.cloned.1.call-update) | async-done | bytes 131088 | tf_op jit(solution)/shard_map/psum | solution.py:194
  730.6 15.4 %all-to-all-start.4 = ((bf16[8,64,128]{2,1,0:T(8,128)(2,1)}), bf16[8,64,128]{2,1,0:T(8,128)(2,1)S(1)}, u32[]{:S(2)}, u32[]{:S(2)}) async-start(bf16[8,64,128]{2,1,0:T(8,128)(2,1)} %get-tuple-element.26), calls=%async_computation.4 | async-start | bytes 262144 | tf_op jit(solution)/shard_map/all_to_all | solution.py:203
  746.0 9.0 %bitcast_convert_fusion = f32[192,2,64,128]{3,2,1,0:T(8,128)} fusion(bf16[64,3,2,64,1,128]{5,3,2,1,4,0:T(8,128)(2,1)} %all-to-all-done.7), kind=kLoop, calls=%fused_computation.5 | loop fusion | flops 3145728 | bytes 18874368 | tf_op jit(solution)/shard_map/convert_element_type | solution.py:191
  755.0 25.2 %scatter_fusion.1 = f32[8,2,64,128]{3,2,1,0:T(8,128)S(1)} fusion(f32[8,2,64,128]{3,2,1,0:T(8,128)S(1)} %copy.149, s32[192]{0:T(256)S(1)} %bitcast.348, f32[192,2,64,128]{3,2,1,0:T(8,128)} %bitcast_convert_fusion), kind=kCustom, calls=%fused_computation.3 | custom fusion | flops 3145728 | bytes 37749504 | tf_op jit(solution)/shard_map/scatter-add | solution.py:190
  781.6 4.8 all-to-all-start.9
  787.1 4.6 all-to-all-done.9
  791.7 4.1 all-to-all-start.8
  796.5 4.6 all-to-all-done.8
  (95 shorter events, 20.6 us)
Async XLA Ops:
  7.2 0.9 copy-start
  8.8 15.4 %all-to-all-start = ((bf16[64,8,128]{2,0,1:T(8,128)(2,1)}), bf16[64,8,128]{2,0,1:T(8,128)(2,1)S(1)}, u32[]{:S(2)}, u32[]{:S(2)}) async-start(bf16[64,8,128]{2,0,1:T(8,128)(2,1)} %copy_bitcast_fusion.7), calls=%async_computation | async-start | bytes 262144 | tf_op jit(solution)/shard_map/all_to_all | solution.py:55
  24.2 9.4 %all-to-all-start.1 = ((bf16[64,8,128]{2,0,1:T(8,128)(2,1)}), bf16[64,8,128]{2,0,1:T(8,128)(2,1)S(1)}, u32[]{:S(2)}, u32[]{:S(2)}) async-start(bf16[64,8,128]{2,0,1:T(8,128)(2,1)} %copy_bitcast_fusion.6), calls=%async_computation.1 | async-start | bytes 262144 | tf_op jit(solution)/shard_map/all_to_all | solution.py:56
  47.6 16.0 %copy-start.3 = (bf16[64,1024]{1,0:T(8,128)(2,1)S(1)}, bf16[64,1024]{1,0:T(8,128)(2,1)}, u32[]{:S(2)}) copy-start(bf16[64,1024]{1,0:T(8,128)(2,1)} %param.6) | copy-start | bytes 393220
  47.6 16.7 %copy-start.4 = (bf16[64,1024]{1,0:T(8,128)(2,1)S(1)}, bf16[64,1024]{1,0:T(8,128)(2,1)}, u32[]{:S(2)}) copy-start(bf16[64,1024]{1,0:T(8,128)(2,1)} %param.9) | copy-start | bytes 393220
  47.6 287.8 %all-to-all-start.2 = ((bf16[64,3,2,64,1,128]{5,3,2,1,4,0:T(8,128)(2,1)}), bf16[64,3,2,64,1,128]{5,3,2,1,4,0:T(8,128)(2,1)}, u32[]{:S(2)}, u32[]{:S(2)}) async-start(bf16[64,3,2,64,1,128]{5,3,2,1,4,0:T(8,128)(2,1)} %broadcast_select_fusion), calls=%async_computation.2 | async-start | bytes 12582912 | tf_op jit(solution)/shard_map/all_to_all | solution.py:86
  335.4 17.5 %all-to-all-start.3 = ((bf16[64,8,128]{2,0,1:T(8,128)(2,1)}), bf16[64,8,128]{2,0,1:T(8,128)(2,1)S(1)}, u32[]{:S(2)}, u32[]{:S(2)}) async-start(bf16[64,8,128]{2,0,1:T(8,128)(2,1)} %copy_bitcast_fusion.5), calls=%async_computation.3 | async-start | bytes 262144 | tf_op jit(solution)/shard_map/all_to_all | solution.py:54
  352.9 10.1 %all-to-all-start.5 = ((bf16[64,8,128]{2,0,1:T(8,128)(2,1)}), bf16[64,8,128]{2,0,1:T(8,128)(2,1)S(1)}, u32[]{:S(2)}, u32[]{:S(2)}) async-start(bf16[64,8,128]{2,0,1:T(8,128)(2,1)} %copy_bitcast_fusion.4), calls=%async_computation.5 | async-start | bytes 262144 | tf_op jit(solution)/shard_map/all_to_all | solution.py:57
  367.8 1.0 copy-start.2
  368.8 6.5 copy-start.1
  369.9 18.3 %all-to-all-start.6 = ((bf16[8,64,128]{2,1,0:T(8,128)(2,1)}), bf16[8,64,128]{2,1,0:T(8,128)(2,1)S(1)}, u32[]{:S(2)}, u32[]{:S(2)}) async-start(bf16[8,64,128]{2,1,0:T(8,128)(2,1)} %fusion.8), calls=%async_computation.6 | async-start | bytes 262144 | tf_op jit(solution)/shard_map/all_to_all | solution.py:204
  375.7 1.7 copy-start.6
  377.5 4.3 copy-start.5
  388.2 6.5 copy-start.7
  388.2 342.4 %all-to-all-start.7 = ((bf16[64,3,2,64,1,128]{5,3,2,1,4,0:T(8,128)(2,1)}), bf16[64,3,2,64,1,128]{5,3,2,1,4,0:T(8,128)(2,1)}, u32[]{:S(2)}, u32[]{:S(2)}) async-start(bf16[64,3,2,64,1,128]{5,3,2,1,4,0:T(8,128)(2,1)} %bitcast.333), calls=%async_computation.7 | async-start | bytes 12582912 | tf_op jit(solution)/shard_map/all_to_all | solution.py:183
  394.7 334.9 %all-reduce.5.cloned.1.call-start = ((), (), s32[]{:S(2)}) async-start(), calls=%async_computation.10 | async-start | bytes 262144 | tf_op jit(solution)/shard_map/psum | solution.py:194
  730.6 51.0 %all-to-all-start.4 = ((bf16[8,64,128]{2,1,0:T(8,128)(2,1)}), bf16[8,64,128]{2,1,0:T(8,128)(2,1)S(1)}, u32[]{:S(2)}, u32[]{:S(2)}) async-start(bf16[8,64,128]{2,1,0:T(8,128)(2,1)} %get-tuple-element.26), calls=%async_computation.4 | async-start | bytes 262144 | tf_op jit(solution)/shard_map/all_to_all | solution.py:203
  781.6 10.1 %all-to-all-start.9 = ((bf16[8,64,128]{2,1,0:T(8,128)(2,1)}), bf16[8,64,128]{2,1,0:T(8,128)(2,1)S(1)}, u32[]{:S(2)}, u32[]{:S(2)}) async-start(bf16[8,64,128]{2,1,0:T(8,128)(2,1)} %get-tuple-element.23), calls=%async_computation.9 | async-start | bytes 262144 | tf_op jit(solution)/shard_map/all_to_all | solution.py:206
  791.7 9.4 %all-to-all-start.8 = ((bf16[8,64,128]{2,1,0:T(8,128)(2,1)}), bf16[8,64,128]{2,1,0:T(8,128)(2,1)S(1)}, u32[]{:S(2)}, u32[]{:S(2)}) async-start(bf16[8,64,128]{2,1,0:T(8,128)(2,1)} %get-tuple-element.24), calls=%async_computation.8 | async-start | bytes 262144 | tf_op jit(solution)/shard_map/all_to_all | solution.py:205
Sparse Core Ops, SparseCore 0:
  399.5 330.0 all-reduce.4
where the time goes:
time: 811 us; the launch traced here: 809 us
  waiting for transfers between devices  620 us (76%)
  starting transfers between devices  78.2 us (10%)
  other arithmetic  54.5 us (7%)
  local copies, waits for them, and re-layouts  30.4 us (4%)
  between operations  14.4 us (2%)
  matrix products  10.7 us (1%)
    psum x1, waiting for transfers between devices, shards(): glob_sums = lax.psum(glob_terms, 'seq')  332 us
    all_to_all x1, waiting for transfers between devices, shards(): lax.all_to_all(outgoing, 'seq', split_axis=0, concat_axis=0, tiled=True)  270 us
    scatter-add x1, other arithmetic, shards(): local_acc.at[send_inner]  25.2 us
  transfers between devices with their start and end apart: 11, of which 7 were waited for; matrix products, arithmetic and copies ran while one was open for 9% of the time, Pallas kernels for 0%

commit v1 on v0

v1 whole, which is shorter than its diff:
```python
import functools

import jax
import jax.numpy as jnp
from jax import lax
from jax.experimental import pallas as pl
from jax.experimental.pallas import tpu as pltpu
from jax.sharding import PartitionSpec as P

HD = 128
BLOCK = 64
QB = 8
NH = 8
NY = 4
NZ = 16
COL = NZ * QB
PLANE = NY * QB
SCALE = HD ** (-0.5)
FLOOR = -1e30
UNROLL = 4
MESH = pl.DeviceIdType.MESH
NT = (((1,), (1,)), ((), ()))
TN = (((0,), (0,)), ((), ()))
NN = (((1,), (0,)), ((), ()))
BF = jnp.bfloat16
F32 = jnp.float32
MIB = 1024 * 1024


def rcopy(src, dst, send, recv, seq, head):
    return pltpu.make_async_remote_copy(
        src_ref=src,
        dst_ref=dst,
        send_sem=send,
        recv_sem=recv,
        device_id=(seq, head),
        device_id_type=MESH,
    )


def place():
    seq = lax.axis_index("seq")
    head = lax.axis_index("head")
    return seq, head, seq // NZ, seq % NZ


def greet(peers):
    barrier = pltpu.get_barrier_semaphore()
    for seq, head in peers:
        pl.semaphore_signal(barrier, inc=1, device_id=(seq, head), device_id_type=MESH)
    pl.semaphore_wait(barrier, len(peers))


def head_peers(seq, head):
    return [(seq, (head + d) % NH) for d in range(1, NH)]


def row_peers(y, z, head):
    return [(((y + d) % NY) * NZ + z, head) for d in range(1, NY)]


def ring_peers(y, z, head):
    return [(y * NZ + (z + 1) % NZ, head), (y * NZ + (z + NZ - 1) % NZ, head)]


def gather_kernel(
    q_ref, k_ref, v_ref, g_ref, kv_ref, qg_ref, kvp, qgp, hs, hr, zs, zr, ys, yr
):
    seq, head, y, z = place()
    greet(head_peers(seq, head) + ring_peers(y, z, head) + row_peers(y, z, head))

    for h in range(NH):
        cols = slice(h * HD, (h + 1) * HD)
        kvp[h, 0] = k_ref[:, cols]
        kvp[h, 1] = v_ref[:, cols]

    def kv_head(d, sender, target):
        return rcopy(
            kvp.at[target], kv_ref.at[z, :, sender], hs.at[0, d - 1], hr.at[0, d - 1], seq, target
        )

    def qg_head(d, sender, target):
        return rcopy(
            qgp.at[target], qg_ref.at[y, :, sender], hs.at[1, d - 1], hr.at[1, d - 1], seq, target
        )

    for d in range(1, NH):
        kv_head(d, head, (head + d) % NH).start()
    kv_ref[z, 0, head] = kvp[head, 0]
    kv_ref[z, 1, head] = kvp[head, 1]
    for h in range(NH):
        cols = slice(h * HD, (h + 1) * HD)
        qgp[h, 0] = q_ref[:, cols]
        qgp[h, 1] = g_ref[:, cols]
    for d in range(1, NH):
        qg_head(d, head, (head + d) % NH).start()
    qg_ref[y, 0, head] = qgp[head, 0]
    qg_ref[y, 1, head] = qgp[head, 1]
    for d in range(1, NH):
        kv_head(d, (head + NH - d) % NH, (head + d) % NH).wait_recv()

    right = y * NZ + (z + 1) % NZ
    left = y * NZ + (z + NZ - 1) % NZ

    def hop(way, step, piece, back):
        if way == 0:
            chunk = (z + 2 * NZ - step - back) % NZ
            target = right
        else:
            chunk = (z + step + back) % NZ
            target = left
        ref = kv_ref.at[chunk, piece]
        return rcopy(ref, ref, zs.at[way, step, piece], zr.at[way, step, piece], target, head)

    half = NZ // 2
    hops = [
        (way, step, piece)
        for step in range(half)
        for piece in range(2)
        for way in range(2)
        if step < half - 1 or piece == way
    ]
    for way, step, piece in hops:
        if step == 0:
            hop(way, step, piece, 0).start()

    def row(d, sender, target):
        ref = qg_ref.at[sender]
        return rcopy(ref, ref, ys.at[d - 1], yr.at[d - 1], target * NZ + z, head)

    for d in range(1, NH):
        qg_head(d, (head + NH - d) % NH, (head + d) % NH).wait_recv()
    for d in range(1, NY):
        row(d, y, (y + d) % NY).start()

    for way, step, piece in hops:
        if step > 0:
            hop(way, step - 1, piece, 1).wait_recv()
            hop(way, step, piece, 0).start()
    for d in range(1, NY):
        row(d, (y + NY - d) % NY, (y + d) % NY).wait_recv()
    for way, step, piece in hops:
        if step == half - 1 or (step == half - 2 and piece != way):
            hop(way, step, piece, 1).wait_recv()
    for d in range(1, NH):
        kv_head(d, head, (head + d) % NH).wait_send()
        qg_head(d, head, (head + d) % NH).wait_send()
    for d in range(1, NY):
        row(d, y, (y + d) % NY).wait_send()
    for way, step, piece in hops:
        hop(way, step, piece, 0).wait_send()


def vmem():
    return pl.BlockSpec(memory_space=pltpu.VMEM)


def smem():
    return pl.BlockSpec(memory_space=pltpu.SMEM)


def gather(q, k, v, g):
    dma = pltpu.SemaphoreType.DMA
    return pl.pallas_call(
        gather_kernel,
        out_shape=(
            jax.ShapeDtypeStruct((NZ, 2, QB, BLOCK, HD), BF),
            jax.ShapeDtypeStruct((NY, 2, QB, BLOCK, HD), BF),
        ),
        in_specs=[vmem()] * 4,
        out_specs=(vmem(), vmem()),
        scratch_shapes=[
            pltpu.VMEM((NH, 2, BLOCK, HD), BF),
            pltpu.VMEM((NH, 2, BLOCK, HD), BF),
            dma((2, NH - 1)),
            dma((2, NH - 1)),
            dma((2, NZ // 2, 2)),
            dma((2, NZ // 2, 2)),
            dma((NY - 1,)),
            dma((NY - 1,)),
        ],
        compiler_params=pltpu.CompilerParams(
            collective_id=0, has_side_effects=True, vmem_limit_bytes=24 * MIB
        ),
        name="gather_rows",
    )(q, k, v, g)


def stats_kernel(ids, gids, kv_ref, qg_ref, st_ref, list_ref, pair_stats):
    y = lax.axis_index("seq") // NZ
    z = lax.axis_index("seq") % NZ
    base = y * COL
    pair_stats[0] = jnp.full((QB + 1, PLANE, BLOCK), FLOOR, F32)
    pair_stats[1] = jnp.zeros((QB + 1, PLANE, BLOCK), F32)
    pair_stats[2] = jnp.zeros((QB + 1, PLANE, BLOCK), F32)

    def note(count, i, slot, block, extra=True):
        rel = block - base
        good = (rel >= 0) & (rel < COL) & extra
        list_ref[count] = (i * QB + slot) * COL + rel
        return count + good.astype(jnp.int32)

    def scan(i, count):
        block = ((i >> 3) * NZ + z) * QB + (i & 7)
        count = note(count, i, 0, block - 1)
        count = note(count, i, 1, block)
        count = note(count, i, 2, block + 1)
        count = note(count, i, 3, gids[0])
        count = note(count, i, 4, gids[1])
        for r in range(3):
            count = note(count, i, 5 + r, ids[block * 3 + r])
        return count

    count = lax.fori_loop(0, PLANE, scan, jnp.int32(0))
    trash = PLANE * QB * COL
    for u in range(UNROLL):
        list_ref[count + u] = jnp.int32(trash)
    rounds = (count + UNROLL - 1) >> 2
    list_ref[PLANE * QB + UNROLL] = rounds

    def pairs(t, carry):
        done = []
        for u in range(UNROLL):
            code = list_ref[t * UNROLL + u]
            pair = code >> 7
            rel = code & (COL - 1)
            i = jnp.minimum(pair >> 3, PLANE - 1)
            live = code < trash
            keys = kv_ref[rel >> 3, 0, rel & 7]
            values = kv_ref[rel >> 3, 1, rel & 7]
            queries = qg_ref[i >> 3, 0, i & 7]
            grads = qg_ref[i >> 3, 1, i & 7]
            scores = lax.dot_general(keys, queries, NT, preferred_element_type=F32) * SCALE
            dprobs = lax.dot_general(values, grads, NT, preferred_element_type=F32)
            top = jnp.max(scores, axis=0, keepdims=True)
            expo = jnp.exp(scores - top)
            total = jnp.sum(expo, axis=0, keepdims=True)
            delta = jnp.sum(expo * dprobs, axis=0, keepdims=True)
            slot = jnp.where(live, pair & (QB - 1), QB)
            done.append((i, slot, top, total, delta))
        for i, slot, top, total, delta in done:
            pair_stats[0, slot, pl.ds(i, 1), :] = top
            pair_stats[1, slot, pl.ds(i, 1), :] = total
            pair_stats[2, slot, pl.ds(i, 1), :] = delta
        return carry

    lax.fori_loop(0, rounds, pairs, 0)
    tops = pair_stats[0, 0:QB]
    top = jnp.max(tops, axis=0)
    factor = jnp.exp(tops - top[None])
    st_ref[0] = top
    st_ref[1] = jnp.sum(pair_stats[1, 0:QB] * factor, axis=0)
    st_ref[2] = jnp.sum(pair_stats[2, 0:QB] * factor, axis=0)


def stats(ids, gids, kv, qg):
    return pl.pallas_call(
        stats_kernel,
        out_shape=(
            jax.ShapeDtypeStruct((3, PLANE, BLOCK), F32),
            jax.ShapeDtypeStruct((PLANE * QB + 2 * UNROLL,), jnp.int32),
        ),
        in_specs=[smem(), smem(), vmem(), vmem()],
        out_specs=(vmem(), smem()),
        scratch_shapes=[pltpu.VMEM((3, QB + 1, PLANE, BLOCK), F32)],
        compiler_params=pltpu.CompilerParams(vmem_limit_bytes=24 * MIB),
        name="pair_stats",
    )(ids, gids, kv, qg)


def share_kernel(st_ref, all_ref, send, recv):
    seq, head, y, z = place()
    greet(row_peers(y, z, head))

    def row(d, sender, target):
        return rcopy(
            st_ref, all_ref.at[sender], send.at[d - 1], recv.at[d - 1], target * NZ + z, head
        )

    for d in range(1, NY):
        row(d, y, (y + d) % NY).start()
    all_ref[y] = st_ref[...]
    for d in range(1, NY):
        row(d, (y + NY - d) % NY, (y + d) % NY).wait_recv()
    for d in range(1, NY):
        row(d, y, (y + d) % NY).wait_send()


def share(st):
    dma = pltpu.SemaphoreType.DMA
    return pl.pallas_call(
        share_kernel,
        out_shape=jax.ShapeDtypeStruct((NY, 3, PLANE, BLOCK), F32),
        in_specs=[vmem()],
        out_specs=vmem(),
        scratch_shapes=[dma((NY - 1,)), dma((NY - 1,))],
        compiler_params=pltpu.CompilerParams(
            collective_id=1, has_side_effects=True, vmem_limit_bytes=8 * MIB
        ),
        name="share_stats",
    )(st)


def terms_kernel(list_ref, all_ref, kv_ref, qg_ref, dkv_ref, oq_ref, row_stats, dkv_acc, oq_acc):
    tops = all_ref[:, 0]
    top = jnp.max(tops, axis=0)
    factor = jnp.exp(tops - top[None])
    inverse = 1.0 / jnp.sum(all_ref[:, 1] * factor, axis=0)
    row_stats[0] = top
    row_stats[1] = inverse
    row_stats[2] = jnp.sum(all_ref[:, 2] * factor, axis=0) * inverse

    def clear_kv(b, carry):
        dkv_acc[b] = jnp.zeros((2, BLOCK, HD), F32)
        return carry

    def clear_oq(b, carry):
        oq_acc[b] = jnp.zeros((2, BLOCK, HD), F32)
        return carry

    lax.fori_loop(0, COL, clear_kv, 0)
    lax.fori_loop(0, PLANE, clear_oq, 0)
    trash = PLANE * QB * COL
    rounds = list_ref[PLANE * QB + UNROLL]

    def pairs(t, carry):
        done = []
        for u in range(UNROLL):
            code = list_ref[t * UNROLL + u]
            pair = code >> 7
            rel = code & (COL - 1)
            live = code < trash
            i = jnp.minimum(pair >> 3, PLANE - 1)
            keys = kv_ref[rel >> 3, 0, rel & 7]
            values = kv_ref[rel >> 3, 1, rel & 7]
            queries = qg_ref[i >> 3, 0, i & 7]
            grads = qg_ref[i >> 3, 1, i & 7]
            scores = lax.dot_general(keys, queries, NT, preferred_element_type=F32) * SCALE
            dprobs = lax.dot_general(values, grads, NT, preferred_element_type=F32)
            weights = jnp.exp(scores - row_stats[0, pl.ds(i, 1), :]) * row_stats[1, pl.ds(i, 1), :]
            probs = weights.astype(BF)
            dscores = (weights * (dprobs - row_stats[2, pl.ds(i, 1), :])).astype(BF)
            dv = lax.dot_general(probs, grads, NN, preferred_element_type=F32)
            dk = lax.dot_general(dscores, queries, NN, preferred_element_type=F32) * SCALE
            out = lax.dot_general(probs, values, TN, preferred_element_type=F32)
            dq = lax.dot_general(dscores, keys, TN, preferred_element_type=F32) * SCALE
            rel = jnp.where(live, rel, COL)
            i = jnp.where(live, i, PLANE)
            done.append((i, rel, dk, dv, out, dq))
        for i, rel, dk, dv, out, dq in done:
            dkv_acc[rel, 0] += dk
            dkv_acc[rel, 1] += dv
            oq_acc[i, 0] += out
            oq_acc[i, 1] += dq
        return carry

    lax.fori_loop(0, rounds, pairs, 0)

    def put_kv(b, carry):
        dkv_ref[b >> 3, 0, b & 7] = dkv_acc[b, 0].astype(BF)
        dkv_ref[b >> 3, 1, b & 7] = dkv_acc[b, 1].astype(BF)
        return carry

    def put_oq(b, carry):
        oq_ref[b >> 3, 0, b & 7] = oq_acc[b, 0].astype(BF)
        oq_ref[b >> 3, 1, b & 7] = oq_acc[b, 1].astype(BF)
        return carry

    lax.fori_loop(0, COL, put_kv, 0)
    lax.fori_loop(0, PLANE, put_oq, 0)


def terms(pair_list, all_stats, kv, qg):
    return pl.pallas_call(
        terms_kernel,
        out_shape=(
            jax.ShapeDtypeStruct((NZ, 2, QB, BLOCK, HD), BF),
            jax.ShapeDtypeStruct((NY, 2, QB, BLOCK, HD), BF),
        ),
        in_specs=[smem(), vmem(), vmem(), vmem()],
        out_specs=(vmem(), vmem()),
        scratch_shapes=[
            pltpu.VMEM((3, PLANE, BLOCK), F32),
            pltpu.VMEM((COL + 1, 2, BLOCK, HD), F32),
            pltpu.VMEM((PLANE + 1, 2, BLOCK, HD), F32),
        ],
        compiler_params=pltpu.CompilerParams(vmem_limit_bytes=40 * MIB),
        name="pair_terms",
    )(pair_list, all_stats, kv, qg)


def reduce_kernel(
    dkv_ref, oq_ref, o_ref, dq_ref, dk_ref, dv_ref, rb, yb, pack, hs, hr, zs, zr, ys, yr
):
    seq, head, y, z = place()
    greet(head_peers(seq, head) + ring_peers(y, z, head) + row_peers(y, z, head))
    right = y * NZ + (z + 1) % NZ
    left = y * NZ + (z + NZ - 1) % NZ
    half = NZ // 2
    outs = (o_ref, dq_ref, dk_ref, dv_ref)

    def chunk_of(way, step):
        if way == 0:
            return (z + half - step) % NZ
        return (z + half + step) % NZ

    def hop(way, step, piece):
        if step == 0 or (step == 1 and piece != way):
            src = dkv_ref.at[chunk_of(way, step), piece]
        else:
            src = rb.at[way, step - 1, piece]
        target = right if way == 0 else left
        return rcopy(
            src,
            rb.at[way, step, piece],
            zs.at[way, step, piece],
            zr.at[way, step, piece],
            target,
            head,
        )

    def row(d, target):
        return rcopy(
            oq_ref.at[target], yb.at[d - 1], ys.at[d - 1], yr.at[d - 1], target * NZ + z, head
        )

    def scatter(a, d, sender, target):
        cols = pl.ds(pl.multiple_of(sender * HD, HD), HD)
        return rcopy(
            pack.at[a, target], outs[a].at[:, cols], hs.at[a, d - 1], hr.at[a, d - 1], seq, target
        )

    def send_heads(a):
        for d in range(1, NH):
            scatter(a, d, head, (head + d) % NH).start()
        cols = pl.ds(pl.multiple_of(head * HD, HD), HD)
        outs[a][:, cols] = pack[a, head]

    hop(0, 0, 0).start()
    hop(1, 0, 1).start()
    for way, piece in ((0, 1), (1, 0)):
        hop(way, 1, piece).start()
    for d in range(1, NY):
        row(d, (y + d) % NY).start()

    for step in range(1, half):
        for piece in range(2):
            for way in range(2):
                if step == 1 and piece != way:
                    continue
                hop(way, step - 1, piece).wait_recv()
                chunk = chunk_of(way, step)

                def add(b, carry, way=way, step=step, piece=piece, chunk=chunk):
                    mine = dkv_ref[chunk, piece, b].astype(F32)
                    rb[way, step - 1, piece, b] = (
                        rb[way, step - 1, piece, b].astype(F32) + mine
                    ).astype(BF)
                    return carry

                lax.fori_loop(0, QB, add, 0)
                hop(way, step, piece).start()
        if step == half - 2:
            for d in range(1, NY):
                row(d, (y + d) % NY).wait_recv()

            def total(b, carry):
                for a in range(2):
                    acc = oq_ref[y, a, b].astype(F32)
                    for d in range(NY - 1):
                        acc = acc + yb[d, a, b].astype(F32)
                    pack[a, b] = acc.astype(BF)
                return carry

            lax.fori_loop(0, QB, total, 0)
            send_heads(0)
            send_heads(1)

    for piece in range(2):
        for way in range(2):
            hop(way, half - 1, piece).wait_recv()

        def last(b, carry, piece=piece):
            acc = dkv_ref[z, piece, b].astype(F32)
            acc = acc + rb[0, half - 1, piece, b].astype(F32)
            acc = acc + rb[1, half - 1, piece, b].astype(F32)
            pack[2 + piece, b] = acc.astype(BF)
            return carry

        lax.fori_loop(0, QB, last, 0)
        send_heads(2 + piece)

    for a in range(4):
        for d in range(1, NH):
            scatter(a, d, (head + NH - d) % NH, (head + d) % NH).wait_recv()
    for a in range(4):
        for d in range(1, NH):
            scatter(a, d, head, (head + d) % NH).wait_send()
    for d in range(1, NY):
        row(d, (y + d) % NY).wait_send()
    for step in range(half):
        for piece in range(2):
            for way in range(2):
                if step > 0 or piece == way:
                    hop(way, step, piece).wait_send()


def reduce(dkv, oq):
    dma = pltpu.SemaphoreType.DMA
    out = jax.ShapeDtypeStruct((BLOCK, NH * HD), BF)
    return pl.pallas_call(
        reduce_kernel,
        out_shape=(out,) * 4,
        in_specs=[vmem()] * 2,
        out_specs=(vmem(),) * 4,
        scratch_shapes=[
            pltpu.VMEM((2, NZ // 2, 2, QB, BLOCK, HD), BF),
            pltpu.VMEM((NY - 1, 2, QB, BLOCK, HD), BF),
            pltpu.VMEM((4, NH, BLOCK, HD), BF),
            dma((4, NH - 1)),
            dma((4, NH - 1)),
            dma((2, NZ // 2, 2)),
            dma((2, NZ // 2, 2)),
            dma((NY - 1,)),
            dma((NY - 1,)),
        ],
        compiler_params=pltpu.CompilerParams(
            collective_id=2, has_side_effects=True, vmem_limit_bytes=32 * MIB
        ),
        name="reduce_rows",
    )(dkv, oq)


def shards(query_rows, key_rows, value_rows, out_grad, random_ids, global_ids):
    kv, qg = gather(query_rows, key_rows, value_rows, out_grad)
    st, pair_list = stats(random_ids.reshape(-1), global_ids, kv, qg)
    dkv, oq = terms(pair_list, share(st), kv, qg)
    return reduce(dkv, oq)


def solution(mesh):
    rows = P(("seq", "head"), None)
    return jax.shard_map(
        shards,
        mesh=mesh,
        in_specs=(rows, rows, rows, rows, P(), P()),
        out_specs=(rows,) * 4,
        check_vma=False,
    )
```

time: 811 us -> 177 us (0.22)
  waiting for transfers between devices: 620 us -> 0 us
  Pallas kernels: 0 us -> 168 us
  starting transfers between devices: 78.2 us -> 0 us
  other arithmetic: 54.5 us -> 0 us
  local copies, waits for them, and re-layouts: 30.4 us -> 7.93 us
  between operations: 14.4 us -> 0.7 us
  matrix products: 10.7 us -> 0 us
    psum x1 -> x0, waiting for transfers between devices: 332 us -> none  [shards(): glob_sums = lax.psum(glob_terms, 'seq')]
    all_to_all x10 -> x0, waiting for transfers between devices: 289 us -> none  [the longest x1 270 us: shards(): lax.all_to_all(outgoing, 'seq', split_axis=0, concat_axis=0, tiled=True)]
    pallas_call x0 -> x5, Pallas kernels: none -> 168 us  [the longest x1 74.4 us: reduce(): pl.pallas_call(reduce_kernel, out_shape=(out,) * 4, in_specs=[vmem()] * 2...]
    all_to_all x10 -> x0, starting transfers between devices: 78.2 us -> none  [the longest x1 15.4 us: shards(): lax.all_to_all(attn_out, 'head', split_axis=0, concat_axis=1, tiled=True)]
    scatter-add x3 -> x0, other arithmetic: 32.3 us -> none  [the longest x1 25.2 us: shards(): local_acc.at[send_inner]]
    gather x2 -> x0, local copies, waits for them, and re-layouts: 11.4 us -> none  [the longest x1 7.9 us: shards(): jnp.take(pair_blk, send_inner, axis=0)]
    dot_general x10 -> x0, matrix products: 10.7 us -> none  [the longest x1 2.74 us: shards(): jnp.einsum('qhbjk,qjkhd->qbhd', prob_bf, value_sel, preferred_element_typ...]
    convert_element_type x3 -> x0, other arithmetic: 10.5 us -> none  [the longest x1 8.98 us: shards(): came_back.reshape((slot_total,) + pair_blk.shape[1:]).astype(jnp.float32)]
  transfers between devices with their start and end apart: 11 -> 0, of which waited for: 7 -> 0; matrix products, arithmetic and copies ran while one was open for 9% -> 0% of each run, Pallas kernels for 0% -> 0%
where the time goes in v1:
time: 177 us
  Pallas kernels  168 us (95%)
  local copies, waits for them, and re-layouts  7.93 us (4%)
    pallas_call x1, Pallas kernels, reduce(): pl.pallas_call(reduce_kernel, out_shape=(out,) * 4, in_specs=[vmem()] * 2...  74.4 us
    pallas_call x1, Pallas kernels, gather(): pl.pallas_call(gather_kernel, out_shape=(jax.ShapeDtypeStruct((NZ, 2, QB,...  65.8 us
    pallas_call x1, Pallas kernels, terms(): pl.pallas_call(terms_kernel, out_shape=(jax.ShapeDtypeStruct((NZ, 2, QB,...  14.1 us
    pallas_call x1, Pallas kernels, share(): pl.pallas_call(share_kernel, out_shape=jax.ShapeDtypeStruct((NY, 3, PLANE...  8.8 us
    unnamed x15, local copies, waits for them, and re-layouts  7.72 us
    pallas_call x1, Pallas kernels, stats(): pl.pallas_call(stats_kernel, out_shape=(jax.ShapeDtypeStruct((3, PLANE, B...  5.13 us

profile of v1, /device:TPU:1, one launch (start us, length us, event | category | flops | bytes accessed | tf_op | source)
XLA Modules:
  0.0 176.8 jit_solution(7458509825662368031)
XLA Ops:
  0.6 0.8 copy.10
  1.5 0.2 reshape.11.ids
  1.7 0.0 copy-start
  1.7 0.9 copy-done
  2.6 0.0 copy-start.1
  2.6 0.9 copy-done.1
  3.5 0.0 copy-start.2
  3.5 0.9 copy-done.2
  4.4 0.0 copy-start.3
  4.4 0.9 copy-done.3
  5.3 65.8 %gather_rows.1 = (bf16[16,2,8,64,128]{4,3,2,1,0:T(8,128)(2,1)S(1)}, bf16[4,2,8,64,128]{4,3,2,1,0:T(8,128)(2,1)S(1)}) custom-call(bf16[64,1024]{1,0:T(8,128)(2,1)S(1)} %copy-done, bf16[64,1024]{1,0:T(8,128)(2,1)S(1)} %copy-done.1, bf16[64,1024]{1,0:T(8,128)(2,1)S(1)} %copy-done.2, bf16[64,1024]{1,0:T(8,128)(2,1)S(1)} %copy-done.3), custom_call_target="tpu_custom_call" | custom-call | tf_op jit(solution)/shard_map/gather_rows/pallas_call | solution.py:164
  71.1 0.0 copy-start.4
  71.1 0.6 copy-done.4
  71.8 5.1 %pair_stats.1 = (f32[3,32,64]{2,1,0:T(8,128)S(1)}, s32[264]{0:T(512)S(1)}) custom-call(s32[1536]{0:T(1024)S(1)} %reshape.11.ids, s32[2]{0:T(128)S(1)} %copy-done.4, bf16[16,2,8,64,128]{4,3,2,1,0:T(8,128)(2,1)S(1)} %get-tuple-element.10.kv_ref, bf16[4,2,8,64,128]{4,3,2,1,0:T(8,128)(2,1)S(1)} %get-tuple-element.11.qg_ref), custom_call_target="tpu_custom_call" | custom-call | tf_op jit(solution)/shard_map/pair_stats/pallas_call | solution.py:257
  76.9 8.8 %share_stats.1.all_ref = f32[4,3,32,64]{3,2,1,0:T(8,128)S(1)} custom-call(f32[3,32,64]{2,1,0:T(8,128)S(1)} %get-tuple-element.13.st_ref), custom_call_target="tpu_custom_call" | custom-call | tf_op jit(solution)/shard_map/share_stats/pallas_call | solution.py:291
  85.7 14.1 %pair_terms.1 = (bf16[16,2,8,64,128]{4,3,2,1,0:T(8,128)(2,1)S(1)}, bf16[4,2,8,64,128]{4,3,2,1,0:T(8,128)(2,1)S(1)}) custom-call(s32[264]{0:T(512)S(1)} %get-tuple-element.12.list_ref, f32[4,3,32,64]{3,2,1,0:T(8,128)S(1)} %share_stats.1.all_ref, bf16[16,2,8,64,128]{4,3,2,1,0:T(8,128)(2,1)S(1)} %get-tuple-element.10.kv_ref, ...), custom_call_target="tpu_custom_call" | custom-call | tf_op jit(solution)/shard_map/pair_terms/pallas_call | solution.py:374
  99.8 74.4 %reduce_rows.1 = (bf16[64,1024]{1,0:T(8,128)(2,1)S(1)}, bf16[64,1024]{1,0:T(8,128)(2,1)S(1)}, bf16[64,1024]{1,0:T(8,128)(2,1)S(1)}, bf16[64,1024]{1,0:T(8,128)(2,1)S(1)}) custom-call(bf16[16,2,8,64,128]{4,3,2,1,0:T(8,128)(2,1)S(1)} %get-tuple-element.14.dkv_ref, bf16[4,2,8,64,128]{4,3,2,1,0:T(8,128)(2,1)S(1)} %get-tuple-element.15.oq_ref), custom_call_target="tpu_custom_call" | custom-call | tf_op jit(solution)/shard_map/reduce_rows/pallas_call | solution.py:511
  174.2 0.7 copy.15
  174.8 0.7 copy.16
  175.5 0.7 copy.17
  176.2 0.7 copy.18
Async XLA Ops:
  1.7 0.9 copy-start
  2.6 0.9 copy-start.1
  3.5 0.9 copy-start.2
  4.4 0.9 copy-start.3
  71.1 0.7 copy-start.4

commit v2 on v1

v2 whole, which is shorter than its diff:
```python
import functools

import jax
import jax.numpy as jnp
from jax import lax
from jax.experimental import pallas as pl
from jax.experimental.pallas import tpu as pltpu
from jax.sharding import PartitionSpec as P

HD = 128
BLOCK = 64
QB = 8
NH = 8
NY = 4
NZ = 16
COL = NZ * QB
PLANE = NY * QB
SCALE = HD ** (-0.5)
FLOOR = -1e30
UNROLL = 4
TILES = PLANE // 4
TRASH = PLANE * 4 * COL
LIST = PLANE * 4 + 8
MESH = pl.DeviceIdType.MESH
NT = (((1,), (1,)), ((), ()))
TN = (((0,), (0,)), ((), ()))
NN = (((1,), (0,)), ((), ()))
BF = jnp.bfloat16
F32 = jnp.float32
MIB = 1024 * 1024


def rcopy(src, dst, send, recv, seq, head):
    return pltpu.make_async_remote_copy(
        src_ref=src,
        dst_ref=dst,
        send_sem=send,
        recv_sem=recv,
        device_id=(seq, head),
        device_id_type=MESH,
    )


def place():
    seq = lax.axis_index("seq")
    head = lax.axis_index("head")
    return seq, head, seq // NZ, seq % NZ


def greet(peers):
    barrier = pltpu.get_barrier_semaphore()
    for seq, head in peers:
        pl.semaphore_signal(barrier, inc=1, device_id=(seq, head), device_id_type=MESH)
    pl.semaphore_wait(barrier, len(peers))


def head_peers(seq, head):
    return [(seq, (head + d) % NH) for d in range(1, NH)]


def row_peers(y, z, head):
    return [(((y + d) % NY) * NZ + z, head) for d in range(1, NY)]


def ring_peers(y, z, head):
    return [(y * NZ + (z + 1) % NZ, head), (y * NZ + (z + NZ - 1) % NZ, head)]


def window_tile(c, kv_ref, qg_ref, y, z):
    lo, hi = max(2 * c - 1, 0), min(2 * c + 3, QB)
    shape = ((hi - lo) * BLOCK, HD)
    keys = kv_ref[z, 0, lo:hi].reshape(shape)
    values = kv_ref[z, 1, lo:hi].reshape(shape)
    queries = qg_ref[y, 0, 2 * c : 2 * c + 2].reshape(2 * BLOCK, HD)
    grads = qg_ref[y, 1, 2 * c : 2 * c + 2].reshape(2 * BLOCK, HD)
    scores = lax.dot_general(keys, queries, NT, preferred_element_type=F32) * SCALE
    dprobs = lax.dot_general(values, grads, NT, preferred_element_type=F32)
    gap = (lo - 2 * c) + (lax.broadcasted_iota(jnp.int32, shape, 0) >> 6)
    gap = gap - (lax.broadcasted_iota(jnp.int32, shape, 1) >> 6)
    near = (gap >= -1) & (gap <= 1)
    return lo, hi, keys, values, queries, grads, jnp.where(near, scores, FLOOR), dprobs


def gather_kernel(
    q_ref, k_ref, v_ref, g_ref, kv_ref, qg_ref, wst_ref, own, hs, hr, zs, zr, ys, yr
):
    seq, head, y, z = place()
    ins = (k_ref, v_ref, q_ref, g_ref)

    def home(a, sender):
        return kv_ref.at[z, a, sender] if a < 2 else qg_ref.at[y, a - 2, sender]

    def cols(h):
        return pl.ds(pl.multiple_of(h * HD, HD), HD)

    def keep(a):
        return pltpu.make_async_copy(ins[a].at[:, cols(head)], home(a, head), own.at[a])

    def give(a, d, sender, target):
        return rcopy(
            ins[a].at[:, cols(target)],
            home(a, sender),
            hs.at[a, d - 1],
            hr.at[a, d - 1],
            seq,
            target,
        )

    def give_all(a):
        for d in range(1, NH):
            give(a, d, head, (head + d) % NH).start()

    def take_all(a):
        for d in range(1, NH):
            give(a, d, (head + NH - d) % NH, (head + d) % NH).wait_recv()
        keep(a).wait()

    for a in range(4):
        keep(a).start()
    greet(head_peers(seq, head) + ring_peers(y, z, head) + row_peers(y, z, head))
    give_all(0)
    give_all(1)

    right = y * NZ + (z + 1) % NZ
    left = y * NZ + (z + NZ - 1) % NZ

    def hop(way, step, piece, back):
        if way == 0:
            chunk = (z + 2 * NZ - step - back) % NZ
            target = right
        else:
            chunk = (z + step + back) % NZ
            target = left
        ref = kv_ref.at[chunk, piece]
        return rcopy(ref, ref, zs.at[way, step, piece], zr.at[way, step, piece], target, head)

    half = NZ // 2
    hops = [
        (way, step, piece)
        for step in range(half)
        for piece in range(2)
        for way in range(2)
        if step < half - 1 or piece == way
    ]
    for piece in range(2):
        take_all(piece)
        for way in range(2):
            hop(way, 0, piece, 0).start()
    give_all(2)
    give_all(3)

    def row(d, sender, target):
        ref = qg_ref.at[sender]
        return rcopy(ref, ref, ys.at[d - 1], yr.at[d - 1], target * NZ + z, head)

    wst_ref[0] = jnp.full((PLANE // 2, HD), FLOOR, F32)
    wst_ref[1] = jnp.zeros((PLANE // 2, HD), F32)
    wst_ref[2] = jnp.zeros((PLANE // 2, HD), F32)

    def window(c):
        _, _, _, _, _, _, scores, dprobs = window_tile(c, kv_ref, qg_ref, y, z)
        top = jnp.max(scores, axis=0, keepdims=True)
        expo = jnp.exp(scores - top)
        at = pl.ds(y * (QB // 2) + c, 1)
        wst_ref[0, at, :] = top
        wst_ref[1, at, :] = jnp.sum(expo, axis=0, keepdims=True)
        wst_ref[2, at, :] = jnp.sum(expo * dprobs, axis=0, keepdims=True)

    for way, step, piece in hops:
        if step == 0:
            continue
        hop(way, step - 1, piece, 1).wait_recv()
        hop(way, step, piece, 0).start()
        if piece == 1 and way == 1:
            if step == 1:
                take_all(2)
                take_all(3)
                for d in range(1, NY):
                    row(d, y, (y + d) % NY).start()
            elif step <= 5:
                window(step - 2)
    for d in range(1, NY):
        row(d, (y + NY - d) % NY, (y + d) % NY).wait_recv()
    for way, step, piece in hops:
        if step == half - 1 or (step == half - 2 and piece != way):
            hop(way, step, piece, 1).wait_recv()
    for a in range(4):
        for d in range(1, NH):
            give(a, d, head, (head + d) % NH).wait_send()
    for d in range(1, NY):
        row(d, y, (y + d) % NY).wait_send()
    for way, step, piece in hops:
        hop(way, step, piece, 0).wait_send()


def vmem():
    return pl.BlockSpec(memory_space=pltpu.VMEM)


def smem():
    return pl.BlockSpec(memory_space=pltpu.SMEM)


def hbm():
    return pl.BlockSpec(memory_space=pltpu.HBM)


def gather(q, k, v, g):
    dma = pltpu.SemaphoreType.DMA
    return pl.pallas_call(
        gather_kernel,
        out_shape=(
            jax.ShapeDtypeStruct((NZ, 2, QB, BLOCK, HD), BF),
            jax.ShapeDtypeStruct((NY, 2, QB, BLOCK, HD), BF),
            jax.ShapeDtypeStruct((3, PLANE // 2, HD), F32),
        ),
        in_specs=[hbm()] * 4,
        out_specs=(vmem(),) * 3,
        scratch_shapes=[
            dma((4,)),
            dma((4, NH - 1)),
            dma((4, NH - 1)),
            dma((2, NZ // 2, 2)),
            dma((2, NZ // 2, 2)),
            dma((NY - 1,)),
            dma((NY - 1,)),
        ],
        compiler_params=pltpu.CompilerParams(
            collective_id=0, has_side_effects=True, vmem_limit_bytes=24 * MIB
        ),
        name="gather_rows",
    )(q, k, v, g)


def stats_kernel(ids, gids, kv_ref, qg_ref, wst_ref, st_ref, list_ref, one, full):
    y = lax.axis_index("seq") // NZ
    z = lax.axis_index("seq") % NZ
    base = y * COL
    one[0] = jnp.full((2, 5, PLANE // 2, HD), FLOOR, F32)
    full[0] = jnp.full((3, PLANE // 2, HD), FLOOR, F32)
    for k in range(1, 3):
        one[k] = jnp.zeros((2, 5, PLANE // 2, HD), F32)
        full[k] = jnp.zeros((3, PLANE // 2, HD), F32)
    for k in range(3):
        full[k, 2] = wst_ref[k]

    def note(count, i, slot, block):
        rel = block - base
        good = (rel >= 0) & (rel < COL)
        list_ref[count] = (i * 4 + slot) * COL + rel
        return count + good.astype(jnp.int32)

    count = jnp.int32(0)
    for g in range(NY):
        first = (g * NZ + z) * QB
        count = note(count, g * QB, 3, first - 1)
        count = note(count, g * QB + QB - 1, 3, first + QB)

        def scan(b, count, g=g, first=first):
            for r in range(3):
                count = note(count, g * QB + b, r, ids[r, first + b])
            return count

        count = lax.fori_loop(0, QB, scan, count, unroll=4)
    for u in range(UNROLL):
        list_ref[count + u] = jnp.int32(TRASH)
    rounds = (count + UNROLL - 1) >> 2
    list_ref[LIST - 1] = rounds

    def pairs(t, carry):
        done = []
        for u in range(UNROLL):
            code = list_ref[t * UNROLL + u]
            pair = code >> 7
            rel = code & (COL - 1)
            i = jnp.minimum(pair >> 2, PLANE - 1)
            keys = kv_ref[rel >> 3, 0, rel & 7]
            values = kv_ref[rel >> 3, 1, rel & 7]
            queries = qg_ref[i >> 3, 0, i & 7]
            grads = qg_ref[i >> 3, 1, i & 7]
            scores = lax.dot_general(keys, queries, NT, preferred_element_type=F32) * SCALE
            dprobs = lax.dot_general(values, grads, NT, preferred_element_type=F32)
            top = jnp.max(scores, axis=0, keepdims=True)
            expo = jnp.exp(scores - top)
            total = jnp.sum(expo, axis=0, keepdims=True)
            delta = jnp.sum(expo * dprobs, axis=0, keepdims=True)
            slot = jnp.where(code < TRASH, pair & 3, 4)
            done.append((i, slot, (top, total, delta)))
        for i, slot, found in done:
            for k in range(3):
                one[k, i & 1, slot, pl.ds(i >> 1, 1), 0:BLOCK] = found[k]
        return carry

    lax.fori_loop(0, rounds, pairs, 0)

    for n in range(2):
        rel = gids[n] - base

        @pl.when((rel >= 0) & (rel < COL))
        def _(n=n, rel=rel):
            keys = kv_ref[rel >> 3, 0, rel & 7]
            values = kv_ref[rel >> 3, 1, rel & 7]
            for t in range(TILES):
                queries, grads = tile_rows(qg_ref, t)
                scores = lax.dot_general(keys, queries, NT, preferred_element_type=F32) * SCALE
                dprobs = lax.dot_general(values, grads, NT, preferred_element_type=F32)
                top = jnp.max(scores, axis=0, keepdims=True)
                expo = jnp.exp(scores - top)
                total = jnp.sum(expo, axis=0, keepdims=True)
                delta = jnp.sum(expo * dprobs, axis=0, keepdims=True)
                for k, found in enumerate((top, total, delta)):
                    for p in range(2):
                        full[k, n, 2 * t + p : 2 * t + p + 1] = found[:, p * HD : (p + 1) * HD]

    def parts(k):
        even = one[k, 0, 0:4]
        odd = pltpu.roll(one[k, 1, 0:4].reshape(2 * PLANE, HD), BLOCK, 1)
        return jnp.concatenate([even, odd.reshape(4, PLANE // 2, HD), full[k]], axis=0)

    tops = parts(0)
    top = jnp.max(tops, axis=0)
    factor = jnp.exp(tops - top[None])
    st_ref[0] = top
    st_ref[1] = jnp.sum(parts(1) * factor, axis=0)
    st_ref[2] = jnp.sum(parts(2) * factor, axis=0)


def tile_rows(qg_ref, t):
    at = slice((t % 2) * 4, (t % 2) * 4 + 4)
    queries = qg_ref[t // 2, 0, at].reshape(4 * BLOCK, HD)
    grads = qg_ref[t // 2, 1, at].reshape(4 * BLOCK, HD)
    return queries, grads


def stats(ids, gids, kv, qg, wst):
    return pl.pallas_call(
        stats_kernel,
        out_shape=(
            jax.ShapeDtypeStruct((3, PLANE // 2, HD), F32),
            jax.ShapeDtypeStruct((LIST,), jnp.int32),
        ),
        in_specs=[smem(), smem(), vmem(), vmem(), vmem()],
        out_specs=(vmem(), smem()),
        scratch_shapes=[
            pltpu.VMEM((3, 2, 5, PLANE // 2, HD), F32),
            pltpu.VMEM((3, 3, PLANE // 2, HD), F32),
        ],
        compiler_params=pltpu.CompilerParams(vmem_limit_bytes=24 * MIB),
        name="pair_stats",
    )(ids, gids, kv, qg, wst)


def share_kernel(st_ref, all_ref, send, recv):
    seq, head, y, z = place()
    greet(row_peers(y, z, head))

    def row(d, sender, target):
        return rcopy(
            st_ref, all_ref.at[sender], send.at[d - 1], recv.at[d - 1], target * NZ + z, head
        )

    for d in range(1, NY):
        row(d, y, (y + d) % NY).start()
    all_ref[y] = st_ref[...]
    for d in range(1, NY):
        row(d, (y + NY - d) % NY, (y + d) % NY).wait_recv()
    for d in range(1, NY):
        row(d, y, (y + d) % NY).wait_send()


def share(st):
    dma = pltpu.SemaphoreType.DMA
    return pl.pallas_call(
        share_kernel,
        out_shape=jax.ShapeDtypeStruct((NY, 3, PLANE // 2, HD), F32),
        in_specs=[vmem()],
        out_specs=vmem(),
        scratch_shapes=[dma((NY - 1,)), dma((NY - 1,))],
        compiler_params=pltpu.CompilerParams(
            collective_id=1, has_side_effects=True, vmem_limit_bytes=8 * MIB
        ),
        name="share_stats",
    )(st)


def terms_kernel(
    list_ref, gids, all_ref, kv_ref, qg_ref, dkv_ref, oq_ref, rows_ref, shifted, oq_acc
):
    base = (lax.axis_index("seq") // NZ) * COL
    tops = all_ref[:, 0]
    top = jnp.max(tops, axis=0)
    factor = jnp.exp(tops - top[None])
    inverse = 1.0 / jnp.sum(all_ref[:, 1] * factor, axis=0)
    delta = jnp.sum(all_ref[:, 2] * factor, axis=0) * inverse
    for k, value in enumerate((top, inverse, delta)):
        rows_ref[k] = value
        shifted[k, 0] = value
        shifted[k, 1] = pltpu.roll(value, BLOCK, 1)

    def clear_kv(b, carry):
        dkv_ref[b] = jnp.zeros((2, QB, BLOCK, HD), BF)
        return carry

    def clear_oq(b, carry):
        oq_acc[b] = jnp.zeros((2, QB, BLOCK, HD), F32)
        return carry

    lax.fori_loop(0, NZ, clear_kv, 0)
    lax.fori_loop(0, NY, clear_oq, 0)
    rounds = list_ref[LIST - 1]

    def add_kv(rel, dk, dv):
        for a, term in enumerate((dk, dv)):
            old = dkv_ref[rel >> 3, a, rel & 7].astype(F32)
            dkv_ref[rel >> 3, a, rel & 7] = (old + term).astype(BF)

    def pairs(t, carry):
        done = []
        for u in range(UNROLL):
            code = list_ref[t * UNROLL + u]
            pair = code >> 7
            rel = code & (COL - 1)
            i = jnp.minimum(pair >> 2, PLANE - 1)
            at = pl.ds(i >> 1, 1)
            keys = kv_ref[rel >> 3, 0, rel & 7]
            values = kv_ref[rel >> 3, 1, rel & 7]
            queries = qg_ref[i >> 3, 0, i & 7]
            grads = qg_ref[i >> 3, 1, i & 7]
            scores = lax.dot_general(keys, queries, NT, preferred_element_type=F32) * SCALE
            dprobs = lax.dot_general(values, grads, NT, preferred_element_type=F32)
            weights = jnp.exp(scores - shifted[0, i & 1, at, 0:BLOCK])
            weights = weights * shifted[1, i & 1, at, 0:BLOCK]
            weights = jnp.where(code < TRASH, weights, 0.0)
            probs = weights.astype(BF)
            dscores = (weights * (dprobs - shifted[2, i & 1, at, 0:BLOCK])).astype(BF)
            dv = lax.dot_general(probs, grads, NN, preferred_element_type=F32)
            dk = lax.dot_general(dscores, queries, NN, preferred_element_type=F32) * SCALE
            out = lax.dot_general(probs, values, TN, preferred_element_type=F32)
            dq = lax.dot_general(dscores, keys, TN, preferred_element_type=F32) * SCALE
            done.append((i, rel, dk, dv, out, dq))
        for i, rel, dk, dv, out, dq in done:
            add_kv(rel, dk, dv)
            oq_acc[i >> 3, 0, i & 7] += out
            oq_acc[i >> 3, 1, i & 7] += dq
        return carry

    lax.fori_loop(0, rounds, pairs, 0)

    for n in range(2):
        rel = gids[n] - base

        @pl.when((rel >= 0) & (rel < COL))
        def _(rel=rel):
            keys = kv_ref[rel >> 3, 0, rel & 7]
            values = kv_ref[rel >> 3, 1, rel & 7]
            dk = jnp.zeros((BLOCK, HD), F32)
            dv = jnp.zeros((BLOCK, HD), F32)
            for t in range(TILES):
                queries, grads = tile_rows(qg_ref, t)

                def wide(k, t=t):
                    pair = [rows_ref[k, 2 * t + p : 2 * t + p + 1] for p in range(2)]
                    return jnp.concatenate(pair, axis=1)

                scores = lax.dot_general(keys, queries, NT, preferred_element_type=F32) * SCALE
                dprobs = lax.dot_general(values, grads, NT, preferred_element_type=F32)
                weights = jnp.exp(scores - wide(0)) * wide(1)
                probs = weights.astype(BF)
                dscores = (weights * (dprobs - wide(2))).astype(BF)
                dv = dv + lax.dot_general(probs, grads, NN, preferred_element_type=F32)
                dk = dk + lax.dot_general(dscores, queries, NN, preferred_element_type=F32) * SCALE
                out = lax.dot_general(probs, values, TN, preferred_element_type=F32)
                dq = lax.dot_general(dscores, keys, TN, preferred_element_type=F32) * SCALE
                at = slice((t % 2) * 4, (t % 2) * 4 + 4)
                oq_acc[t // 2, 0, at] += out.reshape(4, BLOCK, HD)
                oq_acc[t // 2, 1, at] += dq.reshape(4, BLOCK, HD)
            add_kv(rel, dk, dv)

    def put_oq(b, carry):
        oq_ref[b] = oq_acc[b].astype(BF)
        return carry

    lax.fori_loop(0, NY, put_oq, 0)


def terms(pair_list, gids, all_stats, kv, qg):
    return pl.pallas_call(
        terms_kernel,
        out_shape=(
            jax.ShapeDtypeStruct((NZ, 2, QB, BLOCK, HD), BF),
            jax.ShapeDtypeStruct((NY, 2, QB, BLOCK, HD), BF),
            jax.ShapeDtypeStruct((3, PLANE // 2, HD), F32),
        ),
        in_specs=[smem(), smem(), vmem(), vmem(), vmem()],
        out_specs=(vmem(),) * 3,
        scratch_shapes=[
            pltpu.VMEM((3, 2, PLANE // 2, HD), F32),
            pltpu.VMEM((NY, 2, QB, BLOCK, HD), F32),
        ],
        compiler_params=pltpu.CompilerParams(vmem_limit_bytes=32 * MIB),
        name="pair_terms",
    )(pair_list, gids, all_stats, kv, qg)


def reduce_kernel(
    kv_ref,
    qg_ref,
    rows_ref,
    dkv_ref,
    oq_ref,
    o_ref,
    dq_ref,
    dk_ref,
    dv_ref,
    rb,
    yb,
    pack,
    near_kv,
    near_oq,
    hs,
    hr,
    zs,
    zr,
    ys,
    yr,
):
    seq, head, y, z = place()
    greet(head_peers(seq, head) + ring_peers(y, z, head) + row_peers(y, z, head))
    right = y * NZ + (z + 1) % NZ
    left = y * NZ + (z + NZ - 1) % NZ
    half = NZ // 2
    outs = (o_ref, dq_ref, dk_ref, dv_ref)

    def chunk_of(way, step):
        if way == 0:
            return (z + half - step) % NZ
        return (z + half + step) % NZ

    def hop(way, step, piece):
        if step == 0 or (step == 1 and piece != way):
            src = dkv_ref.at[chunk_of(way, step), piece]
        else:
            src = rb.at[way, step - 1, piece]
        target = right if way == 0 else left
        return rcopy(
            src,
            rb.at[way, step, piece],
            zs.at[way, step, piece],
            zr.at[way, step, piece],
            target,
            head,
        )

    def row(d, target):
        return rcopy(
            oq_ref.at[target], yb.at[d - 1], ys.at[d - 1], yr.at[d - 1], target * NZ + z, head
        )

    def scatter(a, d, sender, target):
        cols = pl.ds(pl.multiple_of(sender * HD, HD), HD)
        return rcopy(
            pack.at[a, target], outs[a].at[:, cols], hs.at[a, d - 1], hr.at[a, d - 1], seq, target
        )

    def send_heads(a):
        for d in range(1, NH):
            scatter(a, d, head, (head + d) % NH).start()
        cols = pl.ds(pl.multiple_of(head * HD, HD), HD)
        outs[a][:, cols] = pack[a, head]

    hop(0, 0, 0).start()
    hop(1, 0, 1).start()
    for way, piece in ((0, 1), (1, 0)):
        hop(way, 1, piece).start()
    for d in range(1, NY):
        row(d, (y + d) % NY).start()

    near_kv[...] = jnp.zeros((2, QB, BLOCK, HD), F32)

    def window(c):
        lo, hi, keys, values, queries, grads, scores, dprobs = window_tile(c, kv_ref, qg_ref, y, z)
        at = pl.ds(y * (QB // 2) + c, 1)
        weights = jnp.exp(scores - rows_ref[0, at, :]) * rows_ref[1, at, :]
        probs = weights.astype(BF)
        dscores = (weights * (dprobs - rows_ref[2, at, :])).astype(BF)
        dv = lax.dot_general(probs, grads, NN, preferred_element_type=F32)
        dk = lax.dot_general(dscores, queries, NN, preferred_element_type=F32) * SCALE
        out = lax.dot_general(probs, values, TN, preferred_element_type=F32)
        dq = lax.dot_general(dscores, keys, TN, preferred_element_type=F32) * SCALE
        near_kv[0, lo:hi] += dk.reshape(hi - lo, BLOCK, HD)
        near_kv[1, lo:hi] += dv.reshape(hi - lo, BLOCK, HD)
        near_oq[0, 2 * c : 2 * c + 2] = out.reshape(2, BLOCK, HD)
        near_oq[1, 2 * c : 2 * c + 2] = dq.reshape(2, BLOCK, HD)

    for step in range(1, half):
        for piece in range(2):
            for way in range(2):
                if step == 1 and piece != way:
                    continue
                hop(way, step - 1, piece).wait_recv()
                chunk = chunk_of(way, step)

                def add(b, carry, way=way, step=step, piece=piece, chunk=chunk):
                    mine = dkv_ref[chunk, piece, b].astype(F32)
                    rb[way, step - 1, piece, b] = (
                        rb[way, step - 1, piece, b].astype(F32) + mine
                    ).astype(BF)
                    return carry

                lax.fori_loop(0, QB, add, 0)
                hop(way, step, piece).start()
        if step <= 4:
            window(step - 1)
        if step == half - 2:
            for d in range(1, NY):
                row(d, (y + d) % NY).wait_recv()

            def total(b, carry):
                for a in range(2):
                    acc = near_oq[a, b] + oq_ref[y, a, b].astype(F32)
                    for d in range(NY - 1):
                        acc = acc + yb[d, a, b].astype(F32)
                    pack[a, b] = acc.astype(BF)
                return carry

            lax.fori_loop(0, QB, total, 0)
            send_heads(0)
            send_heads(1)

    for piece in range(2):
        for way in range(2):
            hop(way, half - 1, piece).wait_recv()

        def last(b, carry, piece=piece):
            acc = near_kv[piece, b] + dkv_ref[z, piece, b].astype(F32)
            acc = acc + rb[0, half - 1, piece, b].astype(F32)
            acc = acc + rb[1, half - 1, piece, b].astype(F32)
            pack[2 + piece, b] = acc.astype(BF)
            return carry

        lax.fori_loop(0, QB, last, 0)
        send_heads(2 + piece)

    for a in range(4):
        for d in range(1, NH):
            scatter(a, d, (head + NH - d) % NH, (head + d) % NH).wait_recv()
    for a in range(4):
        for d in range(1, NH):
            scatter(a, d, head, (head + d) % NH).wait_send()
    for d in range(1, NY):
        row(d, (y + d) % NY).wait_send()
    for step in range(half):
        for piece in range(2):
            for way in range(2):
                if step > 0 or piece == way:
                    hop(way, step, piece).wait_send()


def reduce(kv, qg, rows, dkv, oq):
    dma = pltpu.SemaphoreType.DMA
    out = jax.ShapeDtypeStruct((BLOCK, NH * HD), BF)
    return pl.pallas_call(
        reduce_kernel,
        out_shape=(out,) * 4,
        in_specs=[vmem()] * 5,
        out_specs=(vmem(),) * 4,
        scratch_shapes=[
            pltpu.VMEM((2, NZ // 2, 2, QB, BLOCK, HD), BF),
            pltpu.VMEM((NY - 1, 2, QB, BLOCK, HD), BF),
            pltpu.VMEM((4, NH, BLOCK, HD), BF),
            pltpu.VMEM((2, QB, BLOCK, HD), F32),
            pltpu.VMEM((2, QB, BLOCK, HD), F32),
            dma((4, NH - 1)),
            dma((4, NH - 1)),
            dma((2, NZ // 2, 2)),
            dma((2, NZ // 2, 2)),
            dma((NY - 1,)),
            dma((NY - 1,)),
        ],
        compiler_params=pltpu.CompilerParams(
            collective_id=2, has_side_effects=True, vmem_limit_bytes=32 * MIB
        ),
        name="reduce_rows",
    )(kv, qg, rows, dkv, oq)


def deliver_kernel(*refs):
    sems = refs[8]
    copies = [pltpu.make_async_copy(refs[a], refs[4 + a], sems.at[a]) for a in range(4)]
    for copy in copies:
        copy.start()
    for copy in copies:
        copy.wait()


def deliver(outs):
    return pl.pallas_call(
        deliver_kernel,
        out_shape=tuple(jax.ShapeDtypeStruct(o.shape, o.dtype) for o in outs),
        in_specs=[vmem()] * 4,
        out_specs=(hbm(),) * 4,
        scratch_shapes=[pltpu.SemaphoreType.DMA((4,))],
        compiler_params=pltpu.CompilerParams(vmem_limit_bytes=8 * MIB),
        name="deliver_rows",
    )(*outs)


def shards(query_rows, key_rows, value_rows, out_grad, random_ids, global_ids):
    kv, qg, wst = gather(query_rows, key_rows, value_rows, out_grad)
    st, pair_list = stats(random_ids.T, global_ids, kv, qg, wst)
    dkv, oq, rows = terms(pair_list, global_ids, share(st), kv, qg)
    return deliver(reduce(kv, qg, rows, dkv, oq))


def solution(mesh):
    rows = P(("seq", "head"), None)
    return jax.shard_map(
        shards,
        mesh=mesh,
        in_specs=(rows, rows, rows, rows, P(), P()),
        out_specs=(rows,) * 4,
        check_vma=False,
    )
```

time: 177 us -> 150 us (0.85)
  Pallas kernels: 168 us -> 144 us
  local copies, waits for them, and re-layouts: 7.93 us -> 4.97 us
    pallas_call x2 -> x3, Pallas kernels: 79.5 us -> 66 us  [the longest x1 61.5 us: reduce(): pl.pallas_call(reduce_kernel, out_shape=(out,) * 4, in_specs=[vmem()] * 5...]
    pallas_call x1, Pallas kernels: 14.1 us -> 9.11 us  [terms(): pl.pallas_call(terms_kernel, out_shape=(jax.ShapeDtypeStruct((NZ, 2, QB,...]
    pallas_call x1, Pallas kernels: 8.8 us -> 5.29 us  [share(): pl.pallas_call(share_kernel, out_shape=jax.ShapeDtypeStruct((NY, 3, PLANE...]
    unnamed x15 -> x14, local copies, waits for them, and re-layouts: 7.72 us -> 4.97 us
    pallas_call x1, Pallas kernels: 65.8 us -> 63.8 us  [gather(): pl.pallas_call(gather_kernel, out_shape=(jax.ShapeDtypeStruct((NZ, 2, QB,...]
where the time goes in v2:
time: 150 us
  Pallas kernels  144 us (96%)
  local copies, waits for them, and re-layouts  4.97 us (3%)
    pallas_call x1, Pallas kernels, gather(): pl.pallas_call(gather_kernel, out_shape=(jax.ShapeDtypeStruct((NZ, 2, QB,...  63.8 us
    pallas_call x1, Pallas kernels, reduce(): pl.pallas_call(reduce_kernel, out_shape=(out,) * 4, in_specs=[vmem()] * 5...  61.5 us
    pallas_call x1, Pallas kernels, terms(): pl.pallas_call(terms_kernel, out_shape=(jax.ShapeDtypeStruct((NZ, 2, QB,...  9.11 us
    pallas_call x1, Pallas kernels, share(): pl.pallas_call(share_kernel, out_shape=jax.ShapeDtypeStruct((NY, 3, PLANE...  5.29 us
    unnamed x14, local copies, waits for them, and re-layouts  4.97 us
    pallas_call x1, Pallas kernels, stats(): pl.pallas_call(stats_kernel, out_shape=(jax.ShapeDtypeStruct((3, PLANE //...  3.63 us

profile of v2, /device:TPU:1, one launch (start us, length us, event | category | flops | bytes accessed | tf_op | source)
XLA Modules:
  0.0 149.9 jit_solution(3824566543113671540)
XLA Ops:
  0.6 0.0 copy-start.6
  0.6 0.0 copy-start
  0.7 0.9 copy-done
  1.6 0.0 copy-start.1
  1.6 0.9 copy-done.1
  2.5 0.0 copy-start.2
  2.5 0.9 copy-done.2
  3.4 0.0 copy-start.3
  3.4 0.9 copy-done.3
  4.3 63.8 %gather_rows.1 = (bf16[16,2,8,64,128]{4,3,2,1,0:T(8,128)(2,1)S(1)}, bf16[4,2,8,64,128]{4,3,2,1,0:T(8,128)(2,1)S(1)}, f32[3,16,128]{2,1,0:T(8,128)S(1)}) custom-call(bf16[64,1024]{1,0:T(8,128)(2,1)S(1)} %copy-done, bf16[64,1024]{1,0:T(8,128)(2,1)S(1)} %copy-done.1, bf16[64,1024]{1,0:T(8,128)(2,1)S(1)} %copy-done.2, bf16[64,1024]{1,0:T(8,128)(2,1)S(1)} %copy-done.3), custom_call_target="tpu_custom_call" | custom-call | tf_op jit(solution)/shard_map/gather_rows/pallas_call | solution.py:210
  68.1 0.0 copy-start.4
  68.1 0.7 copy-done.4
  68.8 0.0 copy-start.5
  68.8 0.7 copy-done.5
  69.4 3.6 %pair_stats.1 = (f32[3,16,128]{2,1,0:T(8,128)S(1)}, s32[136]{0:T(256)S(1)}) custom-call(s32[3,512]{1,0:T(4,128)S(1)} %bitcast.1, s32[2]{0:T(128)S(1)} %copy-done.5, bf16[16,2,8,64,128]{4,3,2,1,0:T(8,128)(2,1)S(1)} %get-tuple-element.16.kv_ref, bf16[4,2,8,64,128]{4,3,2,1,0:T(8,128)(2,1)S(1)} %get-tuple-element.17.qg_ref, ...), custom_call_target="tpu_custom_call" | custom-call | tf_op jit(solution)/shard_map/pair_stats/pallas_call | solution.py:336
  73.1 5.3 %share_stats.1.all_ref = f32[4,3,16,128]{3,2,1,0:T(8,128)S(1)} custom-call(f32[3,16,128]{2,1,0:T(8,128)S(1)} %get-tuple-element.20.st_ref), custom_call_target="tpu_custom_call" | custom-call | tf_op jit(solution)/shard_map/share_stats/pallas_call | solution.py:373
  78.4 0.0 copy-done.6
  78.4 9.1 %pair_terms.1 = (bf16[16,2,8,64,128]{4,3,2,1,0:T(8,128)(2,1)S(1)}, bf16[4,2,8,64,128]{4,3,2,1,0:T(8,128)(2,1)S(1)}, f32[3,16,128]{2,1,0:T(8,128)S(1)}) custom-call(s32[136]{0:T(256)S(1)} %get-tuple-element.19.list_ref, s32[2]{0:T(128)S(1)} %copy-done.6, f32[4,3,16,128]{3,2,1,0:T(8,128)S(1)} %share_stats.1.all_ref, ...), custom_call_target="tpu_custom_call" | custom-call | tf_op jit(solution)/shard_map/pair_terms/pallas_call | solution.py:487
  87.5 61.5 %reduce_rows.1 = (bf16[64,1024]{1,0:T(8,128)(2,1)S(1)}, bf16[64,1024]{1,0:T(8,128)(2,1)S(1)}, bf16[64,1024]{1,0:T(8,128)(2,1)S(1)}, bf16[64,1024]{1,0:T(8,128)(2,1)S(1)}) custom-call(bf16[16,2,8,64,128]{4,3,2,1,0:T(8,128)(2,1)S(1)} %get-tuple-element.16.kv_ref, bf16[4,2,8,64,128]{4,3,2,1,0:T(8,128)(2,1)S(1)} %get-tuple-element.17.qg_ref, ...), custom_call_target="tpu_custom_call" | custom-call | tf_op jit(solution)/shard_map/reduce_rows/pallas_call | solution.py:662
  149.0 0.8 deliver_rows.1
Async XLA Ops:
  0.6 77.8 %copy-start.6 = (s32[2]{0:T(128)S(1)}, s32[2]{0:T(128)}, u32[]{:S(2)}) copy-start(s32[2]{0:T(128)} %gids.3) | copy-start | bytes 28
  0.6 0.9 copy-start
  1.6 0.9 copy-start.1
  2.5 0.9 copy-start.2
  3.4 0.9 copy-start.3
  68.1 0.7 copy-start.4
  68.8 0.7 copy-start.5

commit v3 on v2

--- a/solution.py
+++ b/solution.py
@@ -384,7 +384,7 @@
 
 
 def terms_kernel(
-    list_ref, gids, all_ref, kv_ref, qg_ref, dkv_ref, oq_ref, rows_ref, shifted, oq_acc
+    list_ref, gids, all_ref, kv_ref, qg_ref, dkv_ref, shifted
 ):
     base = (lax.axis_index("seq") // NZ) * COL
     tops = all_ref[:, 0]
@@ -393,7 +393,6 @@
     inverse = 1.0 / jnp.sum(all_ref[:, 1] * factor, axis=0)
     delta = jnp.sum(all_ref[:, 2] * factor, axis=0) * inverse
     for k, value in enumerate((top, inverse, delta)):
-        rows_ref[k] = value
         shifted[k, 0] = value
         shifted[k, 1] = pltpu.roll(value, BLOCK, 1)
 
@@ -401,12 +400,7 @@
         dkv_ref[b] = jnp.zeros((2, QB, BLOCK, HD), BF)
         return carry
 
-    def clear_oq(b, carry):
-        oq_acc[b] = jnp.zeros((2, QB, BLOCK, HD), F32)
-        return carry
-
     lax.fori_loop(0, NZ, clear_kv, 0)
-    lax.fori_loop(0, NY, clear_oq, 0)
     rounds = list_ref[LIST - 1]
 
     def add_kv(rel, dk, dv):
@@ -435,13 +429,9 @@
             dscores = (weights * (dprobs - shifted[2, i & 1, at, 0:BLOCK])).astype(BF)
             dv = lax.dot_general(probs, grads, NN, preferred_element_type=F32)
             dk = lax.dot_general(dscores, queries, NN, preferred_element_type=F32) * SCALE
-            out = lax.dot_general(probs, values, TN, preferred_element_type=F32)
-            dq = lax.dot_general(dscores, keys, TN, preferred_element_type=F32) * SCALE
-            done.append((i, rel, dk, dv, out, dq))
-        for i, rel, dk, dv, out, dq in done:
+            done.append((rel, dk, dv))
+        for rel, dk, dv in done:
             add_kv(rel, dk, dv)
-            oq_acc[i >> 3, 0, i & 7] += out
-            oq_acc[i >> 3, 1, i & 7] += dq
         return carry
 
     lax.fori_loop(0, rounds, pairs, 0)
@@ -459,7 +449,7 @@
                 queries, grads = tile_rows(qg_ref, t)
 
                 def wide(k, t=t):
-                    pair = [rows_ref[k, 2 * t + p : 2 * t + p + 1] for p in range(2)]
+                    pair = [shifted[k, 0, 2 * t + p : 2 * t + p + 1] for p in range(2)]
                     return jnp.concatenate(pair, axis=1)
 
                 scores = lax.dot_general(keys, queries, NT, preferred_element_type=F32) * SCALE
@@ -469,18 +459,7 @@
                 dscores = (weights * (dprobs - wide(2))).astype(BF)
                 dv = dv + lax.dot_general(probs, grads, NN, preferred_element_type=F32)
                 dk = dk + lax.dot_general(dscores, queries, NN, preferred_element_type=F32) * SCALE
-                out = lax.dot_general(probs, values, TN, preferred_element_type=F32)
-                dq = lax.dot_general(dscores, keys, TN, preferred_element_type=F32) * SCALE
-                at = slice((t % 2) * 4, (t % 2) * 4 + 4)
-                oq_acc[t // 2, 0, at] += out.reshape(4, BLOCK, HD)
-                oq_acc[t // 2, 1, at] += dq.reshape(4, BLOCK, HD)
             add_kv(rel, dk, dv)
-
-    def put_oq(b, carry):
-        oq_ref[b] = oq_acc[b].astype(BF)
-        return carry
-
-    lax.fori_loop(0, NY, put_oq, 0)
 
 
 def terms(pair_list, gids, all_stats, kv, qg):
@@ -488,31 +467,28 @@
         terms_kernel,
         out_shape=(
             jax.ShapeDtypeStruct((NZ, 2, QB, BLOCK, HD), BF),
-            jax.ShapeDtypeStruct((NY, 2, QB, BLOCK, HD), BF),
-            jax.ShapeDtypeStruct((3, PLANE // 2, HD), F32),
+            jax.ShapeDtypeStruct((3, 2, PLANE // 2, HD), F32),
         ),
         in_specs=[smem(), smem(), vmem(), vmem(), vmem()],
-        out_specs=(vmem(),) * 3,
-        scratch_shapes=[
-            pltpu.VMEM((3, 2, PLANE // 2, HD), F32),
-            pltpu.VMEM((NY, 2, QB, BLOCK, HD), F32),
-        ],
+        out_specs=(vmem(),) * 2,
         compiler_params=pltpu.CompilerParams(vmem_limit_bytes=32 * MIB),
         name="pair_terms",
     )(pair_list, gids, all_stats, kv, qg)
 
 
 def reduce_kernel(
+    ids,
+    gids,
     kv_ref,
     qg_ref,
     rows_ref,
     dkv_ref,
-    oq_ref,
     o_ref,
     dq_ref,
     dk_ref,
     dv_ref,
     rb,
+    ob,
     yb,
     pack,
     near_kv,
@@ -529,6 +505,7 @@
     right = y * NZ + (z + 1) % NZ
     left = y * NZ + (z + NZ - 1) % NZ
     half = NZ // 2
+    base = y * COL
     outs = (o_ref, dq_ref, dk_ref, dv_ref)
 
     def chunk_of(way, step):
@@ -553,7 +530,7 @@
 
     def row(d, target):
         return rcopy(
-            oq_ref.at[target], yb.at[d - 1], ys.at[d - 1], yr.at[d - 1], target * NZ + z, head
+            ob.at[d - 1], yb.at[d - 1], ys.at[d - 1], yr.at[d - 1], target * NZ + z, head
         )
 
     def scatter(a, d, sender, target):
@@ -568,29 +545,95 @@
         cols = pl.ds(pl.multiple_of(head * HD, HD), HD)
         outs[a][:, cols] = pack[a, head]
 
-    hop(0, 0, 0).start()
-    hop(1, 0, 1).start()
-    for way, piece in ((0, 1), (1, 0)):
-        hop(way, 1, piece).start()
-    for d in range(1, NY):
-        row(d, (y + d) % NY).start()
-
-    near_kv[...] = jnp.zeros((2, QB, BLOCK, HD), F32)
+    def far(d, b):
+        group = (y + d) % NY
+        first = (group * NZ + z) * QB
+        edge = jnp.where(b == 0, first - 1, jnp.where(b == QB - 1, first + QB, -1))
+        blocks = [ids[r, first + b] for r in range(3)] + [gids[0], gids[1], edge]
+        at = pl.ds(group * (QB // 2) + (b >> 1), 1)
+        top = rows_ref[0, b & 1, at, 0:BLOCK]
+        inverse = rows_ref[1, b & 1, at, 0:BLOCK]
+        delta = rows_ref[2, b & 1, at, 0:BLOCK]
+        rels = [block - base for block in blocks]
+        live = [(rel >= 0) & (rel < COL) for rel in rels]
+        rels = [jnp.clip(rel, 0, COL - 1) for rel in rels]
+        keys = jnp.concatenate([kv_ref[rel >> 3, 0, rel & 7] for rel in rels], axis=0)
+        values = jnp.concatenate([kv_ref[rel >> 3, 1, rel & 7] for rel in rels], axis=0)
+        scores = lax.dot_general(keys, qg_ref[group, 0, b], NT, preferred_element_type=F32)
+        dprobs = lax.dot_general(values, qg_ref[group, 1, b], NT, preferred_element_type=F32)
+        weights = jnp.exp(scores * SCALE - top) * inverse
+        weights = jnp.concatenate(
+            [
+                jnp.where(good, weights[n * BLOCK : (n + 1) * BLOCK], 0.0)
+                for n, good in enumerate(live)
+            ],
+            axis=0,
+        )
+        probs = weights.astype(BF)
+        dscores = (weights * (dprobs - delta)).astype(BF)
+        out = lax.dot_general(probs, values, TN, preferred_element_type=F32)
+        dq = lax.dot_general(dscores, keys, TN, preferred_element_type=F32) * SCALE
+        if d < NY:
+            ob[d - 1, 0, b] = out.astype(BF)
+            ob[d - 1, 1, b] = dq.astype(BF)
+        else:
+            near_oq[0, b] = out
+            near_oq[1, b] = dq
+
+    def far_some(start, count):
+        d = start // QB + 1
+
+        def one(b, carry):
+            far(d, b)
+            return carry
+
+        lax.fori_loop(start % QB, start % QB + count, one, 0, unroll=True)
+        if d < NY and start % QB + count == QB:
+            row(d, (y + d) % NY).start()
 
     def window(c):
         lo, hi, keys, values, queries, grads, scores, dprobs = window_tile(c, kv_ref, qg_ref, y, z)
         at = pl.ds(y * (QB // 2) + c, 1)
-        weights = jnp.exp(scores - rows_ref[0, at, :]) * rows_ref[1, at, :]
+        weights = jnp.exp(scores - rows_ref[0, 0, at, :]) * rows_ref[1, 0, at, :]
         probs = weights.astype(BF)
-        dscores = (weights * (dprobs - rows_ref[2, at, :])).astype(BF)
+        dscores = (weights * (dprobs - rows_ref[2, 0, at, :])).astype(BF)
         dv = lax.dot_general(probs, grads, NN, preferred_element_type=F32)
         dk = lax.dot_general(dscores, queries, NN, preferred_element_type=F32) * SCALE
         out = lax.dot_general(probs, values, TN, preferred_element_type=F32)
         dq = lax.dot_general(dscores, keys, TN, preferred_element_type=F32) * SCALE
         near_kv[0, lo:hi] += dk.reshape(hi - lo, BLOCK, HD)
         near_kv[1, lo:hi] += dv.reshape(hi - lo, BLOCK, HD)
-        near_oq[0, 2 * c : 2 * c + 2] = out.reshape(2, BLOCK, HD)
-        near_oq[1, 2 * c : 2 * c + 2] = dq.reshape(2, BLOCK, HD)
+        near_oq[0, 2 * c : 2 * c + 2] += out.reshape(2, BLOCK, HD)
+        near_oq[1, 2 * c : 2 * c + 2] += dq.reshape(2, BLOCK, HD)
+
+    def total():
+        for d in range(1, NY):
+            row(d, (y + d) % NY).wait_recv()
+
+        def add(b, carry):
+            for a in range(2):
+                acc = near_oq[a, b]
+                for d in range(NY - 1):
+                    acc = acc + yb[d, a, b].astype(F32)
+                pack[a, b] = acc.astype(BF)
+            return carry
+
+        lax.fori_loop(0, QB, add, 0)
+        send_heads(0)
+        send_heads(1)
+
+    jobs = [functools.partial(far_some, n, 2) for n in range(6, NY * QB, 2)]
+    for c in range(QB // 2):
+        jobs += [functools.partial(window, c)]
+    jobs += [lambda: None] * 2 + [total]
+
+    hop(0, 0, 0).start()
+    hop(1, 0, 1).start()
+    for way, piece in ((0, 1), (1, 0)):
+        hop(way, 1, piece).start()
+    near_kv[...] = jnp.zeros((2, QB, BLOCK, HD), F32)
+    for n in range(0, 6, 2):
+        far_some(n, 2)
 
     for step in range(1, half):
         for piece in range(2):
@@ -609,23 +652,10 @@
 
                 lax.fori_loop(0, QB, add, 0)
                 hop(way, step, piece).start()
-        if step <= 4:
-            window(step - 1)
-        if step == half - 2:
-            for d in range(1, NY):
-                row(d, (y + d) % NY).wait_recv()
-
-            def total(b, carry):
-                for a in range(2):
-                    acc = near_oq[a, b] + oq_ref[y, a, b].astype(F32)
-                    for d in range(NY - 1):
-                        acc = acc + yb[d, a, b].astype(F32)
-                    pack[a, b] = acc.astype(BF)
-                return carry
-
-            lax.fori_loop(0, QB, total, 0)
-            send_heads(0)
-            send_heads(1)
+                if jobs:
+                    jobs.pop(0)()
+    for job in jobs:
+        job()
 
     for piece in range(2):
         for way in range(2):
@@ -656,16 +686,17 @@
                     hop(way, step, piece).wait_send()
 
 
-def reduce(kv, qg, rows, dkv, oq):
+def reduce(ids, gids, kv, qg, rows, dkv):
     dma = pltpu.SemaphoreType.DMA
     out = jax.ShapeDtypeStruct((BLOCK, NH * HD), BF)
     return pl.pallas_call(
         reduce_kernel,
         out_shape=(out,) * 4,
-        in_specs=[vmem()] * 5,
+        in_specs=[smem()] * 2 + [vmem()] * 4,
         out_specs=(vmem(),) * 4,
         scratch_shapes=[
             pltpu.VMEM((2, NZ // 2, 2, QB, BLOCK, HD), BF),
+            pltpu.VMEM((NY - 1, 2, QB, BLOCK, HD), BF),
             pltpu.VMEM((NY - 1, 2, QB, BLOCK, HD), BF),
             pltpu.VMEM((4, NH, BLOCK, HD), BF),
             pltpu.VMEM((2, QB, BLOCK, HD), F32),
@@ -681,7 +712,7 @@
             collective_id=2, has_side_effects=True, vmem_limit_bytes=32 * MIB
         ),
         name="reduce_rows",
-    )(kv, qg, rows, dkv, oq)
+    )(ids, gids, kv, qg, rows, dkv)
 
 
 def deliver_kernel(*refs):
@@ -706,10 +737,13 @@
 
 
 def shards(query_rows, key_rows, value_rows, out_grad, random_ids, global_ids):
-    kv, qg, wst = gather(query_rows, key_rows, value_rows, out_grad)
-    st, pair_list = stats(random_ids.T, global_ids, kv, qg, wst)
-    dkv, oq, rows = terms(pair_list, global_ids, share(st), kv, qg)
-    return deliver(reduce(kv, qg, rows, dkv, oq))
+    rows = (query_rows, key_rows, value_rows, out_grad)
+    kv, qg, wst = gather(*(pltpu.with_memory_space_constraint(r, pltpu.HBM) for r in rows))
+    ids = pltpu.with_memory_space_constraint(random_ids.T, pltpu.HBM)
+    global_ids = pltpu.with_memory_space_constraint(global_ids, pltpu.HBM)
+    st, pair_list = stats(ids, global_ids, kv, qg, wst)
+    dkv, row_stats = terms(pair_list, global_ids, share(st), kv, qg)
+    return deliver(reduce(ids, global_ids, kv, qg, row_stats, dkv))
 
 
 def solution(mesh):

time: 150 us -> 143 us (0.953)
  local copies, waits for them, and re-layouts: 4.97 us -> 0 us
  Pallas kernels: 144 us -> 142 us
    unnamed x14 -> x0, local copies, waits for them, and re-layouts: 4.97 us -> none
    pallas_call x1, Pallas kernels: 9.11 us -> 6.58 us  [terms(): pl.pallas_call(terms_kernel, out_shape=(jax.ShapeDtypeStruct((NZ, 2, QB,...]
where the time goes in v3:
time: 143 us; the launch traced here: 142 us
  Pallas kernels  142 us (99%)
    pallas_call x1, Pallas kernels, gather(): pl.pallas_call(gather_kernel, out_shape=(jax.ShapeDtypeStruct((NZ, 2, QB,...  64 us
    pallas_call x1, Pallas kernels, reduce(): pl.pallas_call(reduce_kernel, out_shape=(out,) * 4, in_specs=[smem()] * 2...  61.1 us
    pallas_call x1, Pallas kernels, terms(): pl.pallas_call(terms_kernel, out_shape=(jax.ShapeDtypeStruct((NZ, 2, QB,...  6.58 us
    pallas_call x1, Pallas kernels, share(): pl.pallas_call(share_kernel, out_shape=jax.ShapeDtypeStruct((NY, 3, PLANE...  5.48 us
    pallas_call x1, Pallas kernels, stats(): pl.pallas_call(stats_kernel, out_shape=(jax.ShapeDtypeStruct((3, PLANE //...  3.58 us

profile of v3, /device:TPU:1, one launch (start us, length us, event | category | flops | bytes accessed | tf_op | source)
XLA Modules:
  0.0 142.4 jit_solution(14816465736932046250)
XLA Ops:
  0.6 64.0 %gather_rows.1 = (bf16[16,2,8,64,128]{4,3,2,1,0:T(8,128)(2,1)S(1)}, bf16[4,2,8,64,128]{4,3,2,1,0:T(8,128)(2,1)S(1)}, f32[3,16,128]{2,1,0:T(8,128)S(1)}) custom-call(bf16[64,1024]{1,0:T(8,128)(2,1)} %q_ref.1, bf16[64,1024]{1,0:T(8,128)(2,1)} %k_ref.1, bf16[64,1024]{1,0:T(8,128)(2,1)} %v_ref.1, bf16[64,1024]{1,0:T(8,128)(2,1)} %g_ref.1), custom_call_target="tpu_custom_call" | custom-call | tf_op jit(solution)/shard_map/gather_rows/pallas_call | solution.py:210
  64.7 3.6 %pair_stats.1 = (f32[3,16,128]{2,1,0:T(8,128)S(1)}, s32[136]{0:T(256)S(1)}) custom-call(s32[3,512]{1,0:T(4,128)} %bitcast.1, s32[2]{0:T(128)} %gids.5, bf16[16,2,8,64,128]{4,3,2,1,0:T(8,128)(2,1)S(1)} %get-tuple-element.15.kv_ref, bf16[4,2,8,64,128]{4,3,2,1,0:T(8,128)(2,1)S(1)} %get-tuple-element.16.qg_ref, f32[3,16,128]{2,1,0:T(8,128)S(1)} %get-tuple-element.17.wst_ref), custom_call_target="tpu_custom_call" | custom-call | tf_op jit(solution)/shard_map/pair_stats/pallas_call | solution.py:336
  68.3 5.5 %share_stats.1.all_ref = f32[4,3,16,128]{3,2,1,0:T(8,128)S(1)} custom-call(f32[3,16,128]{2,1,0:T(8,128)S(1)} %get-tuple-element.19.st_ref), custom_call_target="tpu_custom_call" | custom-call | tf_op jit(solution)/shard_map/share_stats/pallas_call | solution.py:373
  73.8 6.6 %pair_terms.1 = (bf16[16,2,8,64,128]{4,3,2,1,0:T(8,128)(2,1)S(1)}, f32[3,2,16,128]{3,2,1,0:T(8,128)S(1)}) custom-call(s32[136]{0:T(256)S(1)} %get-tuple-element.18.list_ref, s32[2]{0:T(128)} %gids.5, f32[4,3,16,128]{3,2,1,0:T(8,128)S(1)} %share_stats.1.all_ref, bf16[16,2,8,64,128]{4,3,2,1,0:T(8,128)(2,1)S(1)} %get-tuple-element.15.kv_ref, ...), custom_call_target="tpu_custom_call" | custom-call | tf_op jit(solution)/shard_map/pair_terms/pallas_call | solution.py:466
  80.3 61.1 %reduce_rows.1 = (bf16[64,1024]{1,0:T(8,128)(2,1)S(1)}, bf16[64,1024]{1,0:T(8,128)(2,1)S(1)}, bf16[64,1024]{1,0:T(8,128)(2,1)S(1)}, bf16[64,1024]{1,0:T(8,128)(2,1)S(1)}) custom-call(s32[3,512]{1,0:T(4,128)} %bitcast.2, s32[2]{0:T(128)} %gids.5, bf16[16,2,8,64,128]{4,3,2,1,0:T(8,128)(2,1)S(1)} %get-tuple-element.15.kv_ref, ...), custom_call_target="tpu_custom_call" | custom-call | tf_op jit(solution)/shard_map/reduce_rows/pallas_call | solution.py:692
  141.5 0.8 deliver_rows.1

commit v4 on v3

--- a/solution.py
+++ b/solution.py
@@ -17,10 +17,12 @@
 PLANE = NY * QB
 SCALE = HD ** (-0.5)
 FLOOR = -1e30
-UNROLL = 4
+UNROLL = 8
+TURNS = (4, 3, 5, 2, 6, 1, 7, 0)
 TILES = PLANE // 4
 TRASH = PLANE * 4 * COL
-LIST = PLANE * 4 + 8
+LIST = PLANE * 4 + 16
+PAIRS = PLANE * 3 + 2 * NY + 8
 MESH = pl.DeviceIdType.MESH
 NT = (((1,), (1,)), ((), ()))
 TN = (((0,), (0,)), ((), ()))
@@ -60,10 +62,6 @@
 
 def row_peers(y, z, head):
     return [(((y + d) % NY) * NZ + z, head) for d in range(1, NY)]
-
-
-def ring_peers(y, z, head):
-    return [(y * NZ + (z + 1) % NZ, head), (y * NZ + (z + NZ - 1) % NZ, head)]
 
 
 def window_tile(c, kv_ref, qg_ref, y, z):
@@ -81,8 +79,12 @@
     return lo, hi, keys, values, queries, grads, jnp.where(near, scores, FLOOR), dprobs
 
 
+def near_planes(y, z):
+    return [(y * NZ + (z + d) % NZ, h) for d in (1, NZ - 1) for h in range(NH)]
+
+
 def gather_kernel(
-    q_ref, k_ref, v_ref, g_ref, kv_ref, qg_ref, wst_ref, own, hs, hr, zs, zr, ys, yr
+    q_ref, k_ref, v_ref, g_ref, kv_ref, qg_ref, wst_ref, own, hs, hr, fs, fr, zs, zr, ys, yr
 ):
     seq, head, y, z = place()
     ins = (k_ref, v_ref, q_ref, g_ref)
@@ -117,38 +119,54 @@
 
     for a in range(4):
         keep(a).start()
-    greet(head_peers(seq, head) + ring_peers(y, z, head) + row_peers(y, z, head))
-    give_all(0)
-    give_all(1)
-
+    greet(head_peers(seq, head) + near_planes(y, z) + row_peers(y, z, head))
     right = y * NZ + (z + 1) % NZ
     left = y * NZ + (z + NZ - 1) % NZ
+    sides = (right, left)
+
+    def first(way, piece, d):
+        target = (head + d) % NH
+        return rcopy(
+            ins[piece].at[:, cols(target)],
+            kv_ref.at[z, piece, head],
+            fs.at[way, piece, d],
+            fr.at[way, piece, d],
+            sides[way],
+            target,
+        )
+
+    def first_in(way, piece, d):
+        sender = (head + NH - d) % NH
+        chunk = (z + NZ - 1 + 2 * way) % NZ
+        return rcopy(
+            ins[piece].at[:, cols(head)],
+            kv_ref.at[chunk, piece, sender],
+            fs.at[way, piece, d],
+            fr.at[way, piece, d],
+            sides[way],
+            sender,
+        )
 
     def hop(way, step, piece, back):
         if way == 0:
             chunk = (z + 2 * NZ - step - back) % NZ
-            target = right
         else:
             chunk = (z + step + back) % NZ
-            target = left
         ref = kv_ref.at[chunk, piece]
-        return rcopy(ref, ref, zs.at[way, step, piece], zr.at[way, step, piece], target, head)
+        return rcopy(ref, ref, zs.at[way, step, piece], zr.at[way, step, piece], sides[way], head)
 
     half = NZ // 2
     hops = [
         (way, step, piece)
-        for step in range(half)
+        for step in range(1, half)
         for piece in range(2)
         for way in range(2)
         if step < half - 1 or piece == way
     ]
     for piece in range(2):
-        take_all(piece)
-        for way in range(2):
-            hop(way, 0, piece, 0).start()
-    give_all(2)
-    give_all(3)
-
+        for d in TURNS:
+            for way in range(2):
+                first(way, piece, d).start()
     def row(d, sender, target):
         ref = qg_ref.at[sender]
         return rcopy(ref, ref, ys.at[d - 1], yr.at[d - 1], target * NZ + z, head)
@@ -167,18 +185,23 @@
         wst_ref[2, at, :] = jnp.sum(expo * dprobs, axis=0, keepdims=True)
 
     for way, step, piece in hops:
-        if step == 0:
-            continue
-        hop(way, step - 1, piece, 1).wait_recv()
+        if step == 1:
+            for d in range(NH):
+                first_in(way, piece, d).wait_recv()
+        else:
+            hop(way, step - 1, piece, 1).wait_recv()
         hop(way, step, piece, 0).start()
         if piece == 1 and way == 1:
             if step == 1:
-                take_all(2)
-                take_all(3)
+                for a in (2, 3, 0, 1):
+                    give_all(a)
+            elif step == 3:
+                for a in range(4):
+                    take_all(a)
                 for d in range(1, NY):
                     row(d, y, (y + d) % NY).start()
-            elif step <= 5:
-                window(step - 2)
+            elif step >= 4:
+                window(step - 4)
     for d in range(1, NY):
         row(d, (y + NY - d) % NY, (y + d) % NY).wait_recv()
     for way, step, piece in hops:
@@ -189,6 +212,10 @@
             give(a, d, head, (head + d) % NH).wait_send()
     for d in range(1, NY):
         row(d, y, (y + d) % NY).wait_send()
+    for way in range(2):
+        for piece in range(2):
+            for d in range(NH):
+                first(way, piece, d).wait_send()
     for way, step, piece in hops:
         hop(way, step, piece, 0).wait_send()
 
@@ -220,6 +247,8 @@
             dma((4,)),
             dma((4, NH - 1)),
             dma((4, NH - 1)),
+            dma((2, 2, NH)),
+            dma((2, 2, NH)),
             dma((2, NZ // 2, 2)),
             dma((2, NZ // 2, 2)),
             dma((NY - 1,)),
@@ -232,7 +261,9 @@
     )(q, k, v, g)
 
 
-def stats_kernel(ids, gids, kv_ref, qg_ref, wst_ref, st_ref, list_ref, one, full):
+def stats_kernel(
+    ids, gids, kv_ref, qg_ref, wst_ref, st_ref, list_ref, one, expo_ref, dprob_ref, full
+):
     y = lax.axis_index("seq") // NZ
     z = lax.axis_index("seq") % NZ
     base = y * COL
@@ -264,7 +295,7 @@
         count = lax.fori_loop(0, QB, scan, count, unroll=4)
     for u in range(UNROLL):
         list_ref[count + u] = jnp.int32(TRASH)
-    rounds = (count + UNROLL - 1) >> 2
+    rounds = (count + UNROLL - 1) >> 3
     list_ref[LIST - 1] = rounds
 
     def pairs(t, carry):
@@ -285,8 +316,10 @@
             total = jnp.sum(expo, axis=0, keepdims=True)
             delta = jnp.sum(expo * dprobs, axis=0, keepdims=True)
             slot = jnp.where(code < TRASH, pair & 3, 4)
-            done.append((i, slot, (top, total, delta)))
-        for i, slot, found in done:
+            done.append((i, slot, (top, total, delta), expo, dprobs))
+        for u, (i, slot, found, expo, dprobs) in enumerate(done):
+            expo_ref[t * UNROLL + u] = expo
+            dprob_ref[t * UNROLL + u] = dprobs
             for k in range(3):
                 one[k, i & 1, slot, pl.ds(i >> 1, 1), 0:BLOCK] = found[k]
         return carry
@@ -338,11 +371,13 @@
         out_shape=(
             jax.ShapeDtypeStruct((3, PLANE // 2, HD), F32),
             jax.ShapeDtypeStruct((LIST,), jnp.int32),
+            jax.ShapeDtypeStruct((3, 2, 5, PLANE // 2, HD), F32),
+            jax.ShapeDtypeStruct((PAIRS, BLOCK, BLOCK), F32),
+            jax.ShapeDtypeStruct((PAIRS, BLOCK, BLOCK), F32),
         ),
         in_specs=[smem(), smem(), vmem(), vmem(), vmem()],
-        out_specs=(vmem(), smem()),
+        out_specs=(vmem(), smem(), vmem(), vmem(), vmem()),
         scratch_shapes=[
-            pltpu.VMEM((3, 2, 5, PLANE // 2, HD), F32),
             pltpu.VMEM((3, 3, PLANE // 2, HD), F32),
         ],
         compiler_params=pltpu.CompilerParams(vmem_limit_bytes=24 * MIB),
@@ -384,7 +419,7 @@
 
 
 def terms_kernel(
-    list_ref, gids, all_ref, kv_ref, qg_ref, dkv_ref, shifted
+    list_ref, gids, all_ref, kv_ref, qg_ref, one, expo_ref, dprob_ref, dkv_ref, shifted, scale_ref
 ):
     base = (lax.axis_index("seq") // NZ) * COL
     tops = all_ref[:, 0]
@@ -396,6 +431,11 @@
         shifted[k, 0] = value
         shifted[k, 1] = pltpu.roll(value, BLOCK, 1)
 
+    for p in range(2):
+        factor = jnp.exp(one[0, p, 0:4] - shifted[0, p][None]) * shifted[1, p][None]
+        scale_ref[p, 0:4] = factor
+        scale_ref[p, 4] = jnp.zeros((PLANE // 2, HD), F32)
+
     def clear_kv(b, carry):
         dkv_ref[b] = jnp.zeros((2, QB, BLOCK, HD), BF)
         return carry
@@ -416,15 +456,11 @@
             rel = code & (COL - 1)
             i = jnp.minimum(pair >> 2, PLANE - 1)
             at = pl.ds(i >> 1, 1)
-            keys = kv_ref[rel >> 3, 0, rel & 7]
-            values = kv_ref[rel >> 3, 1, rel & 7]
+            slot = jnp.where(code < TRASH, pair & 3, 4)
             queries = qg_ref[i >> 3, 0, i & 7]
             grads = qg_ref[i >> 3, 1, i & 7]
-            scores = lax.dot_general(keys, queries, NT, preferred_element_type=F32) * SCALE
-            dprobs = lax.dot_general(values, grads, NT, preferred_element_type=F32)
-            weights = jnp.exp(scores - shifted[0, i & 1, at, 0:BLOCK])
-            weights = weights * shifted[1, i & 1, at, 0:BLOCK]
-            weights = jnp.where(code < TRASH, weights, 0.0)
+            weights = expo_ref[t * UNROLL + u] * scale_ref[i & 1, slot, at, 0:BLOCK]
+            dprobs = dprob_ref[t * UNROLL + u]
             probs = weights.astype(BF)
             dscores = (weights * (dprobs - shifted[2, i & 1, at, 0:BLOCK])).astype(BF)
             dv = lax.dot_general(probs, grads, NN, preferred_element_type=F32)
@@ -462,18 +498,19 @@
             add_kv(rel, dk, dv)
 
 
-def terms(pair_list, gids, all_stats, kv, qg):
+def terms(pair_list, gids, all_stats, kv, qg, pairs):
     return pl.pallas_call(
         terms_kernel,
         out_shape=(
             jax.ShapeDtypeStruct((NZ, 2, QB, BLOCK, HD), BF),
             jax.ShapeDtypeStruct((3, 2, PLANE // 2, HD), F32),
         ),
-        in_specs=[smem(), smem(), vmem(), vmem(), vmem()],
+        in_specs=[smem(), smem()] + [vmem()] * 6,
         out_specs=(vmem(),) * 2,
+        scratch_shapes=[pltpu.VMEM((2, 5, PLANE // 2, HD), F32)],
         compiler_params=pltpu.CompilerParams(vmem_limit_bytes=32 * MIB),
         name="pair_terms",
-    )(pair_list, gids, all_stats, kv, qg)
+    )(pair_list, gids, all_stats, kv, qg, *pairs)
 
 
 def reduce_kernel(
@@ -493,15 +530,18 @@
     pack,
     near_kv,
     near_oq,
+    fin,
     hs,
     hr,
+    fs,
+    fr,
     zs,
     zr,
     ys,
     yr,
 ):
     seq, head, y, z = place()
-    greet(head_peers(seq, head) + ring_peers(y, z, head) + row_peers(y, z, head))
+    greet(head_peers(seq, head) + near_planes(y, z) + row_peers(y, z, head))
     right = y * NZ + (z + 1) % NZ
     left = y * NZ + (z + NZ - 1) % NZ
     half = NZ // 2
@@ -533,17 +573,30 @@
             ob.at[d - 1], yb.at[d - 1], ys.at[d - 1], yr.at[d - 1], target * NZ + z, head
         )
 
+    def cols(h):
+        return pl.ds(pl.multiple_of(h * HD, HD), HD)
+
     def scatter(a, d, sender, target):
-        cols = pl.ds(pl.multiple_of(sender * HD, HD), HD)
-        return rcopy(
-            pack.at[a, target], outs[a].at[:, cols], hs.at[a, d - 1], hr.at[a, d - 1], seq, target
-        )
+        home = outs[a].at[:, cols(sender)] if a < 2 else fin.at[2, a - 2, sender]
+        return rcopy(pack.at[a, target], home, hs.at[a, d - 1], hr.at[a, d - 1], seq, target)
 
     def send_heads(a):
         for d in range(1, NH):
             scatter(a, d, head, (head + d) % NH).start()
-        cols = pl.ds(pl.multiple_of(head * HD, HD), HD)
-        outs[a][:, cols] = pack[a, head]
+        if a < 2:
+            outs[a][:, cols(head)] = pack[a, head]
+        else:
+            fin[2, a - 2, head] = pack[a, head]
+
+    def final(way, piece, d, sender, target):
+        return rcopy(
+            rb.at[way, half - 2, piece, target],
+            fin.at[way, piece, sender],
+            fs.at[way, piece, d],
+            fr.at[way, piece, d],
+            right if way == 0 else left,
+            target,
+        )
 
     def far(d, b):
         group = (y + d) % NY
@@ -622,10 +675,21 @@
         send_heads(0)
         send_heads(1)
 
+    def give_near():
+        def add(b, carry):
+            for piece in range(2):
+                acc = near_kv[piece, b] + dkv_ref[z, piece, b].astype(F32)
+                pack[2 + piece, b] = acc.astype(BF)
+            return carry
+
+        lax.fori_loop(0, QB, add, 0)
+        send_heads(2)
+        send_heads(3)
+
     jobs = [functools.partial(far_some, n, 2) for n in range(6, NY * QB, 2)]
     for c in range(QB // 2):
         jobs += [functools.partial(window, c)]
-    jobs += [lambda: None] * 2 + [total]
+    jobs += [give_near, lambda: None, total]
 
     hop(0, 0, 0).start()
     hop(1, 0, 1).start()
@@ -651,35 +715,40 @@
                     return carry
 
                 lax.fori_loop(0, QB, add, 0)
-                hop(way, step, piece).start()
+                if step < half - 1:
+                    hop(way, step, piece).start()
+                else:
+                    for d in TURNS:
+                        final(way, piece, d, head, (head + d) % NH).start()
                 if jobs:
                     jobs.pop(0)()
     for job in jobs:
         job()
 
-    for piece in range(2):
-        for way in range(2):
-            hop(way, half - 1, piece).wait_recv()
-
-        def last(b, carry, piece=piece):
-            acc = near_kv[piece, b] + dkv_ref[z, piece, b].astype(F32)
-            acc = acc + rb[0, half - 1, piece, b].astype(F32)
-            acc = acc + rb[1, half - 1, piece, b].astype(F32)
-            pack[2 + piece, b] = acc.astype(BF)
-            return carry
-
-        lax.fori_loop(0, QB, last, 0)
-        send_heads(2 + piece)
-
     for a in range(4):
         for d in range(1, NH):
             scatter(a, d, (head + NH - d) % NH, (head + d) % NH).wait_recv()
+    for piece in range(2):
+        for way in range(2):
+            for d in range(NH):
+                final(way, piece, d, (head + NH - d) % NH, (head + d) % NH).wait_recv()
+
+        for h in range(NH):
+            acc = fin[2, piece, h].astype(F32)
+            acc = acc + fin[0, piece, h].astype(F32)
+            acc = acc + fin[1, piece, h].astype(F32)
+            outs[2 + piece][:, h * HD : (h + 1) * HD] = acc.astype(BF)
+
     for a in range(4):
         for d in range(1, NH):
             scatter(a, d, head, (head + d) % NH).wait_send()
     for d in range(1, NY):
         row(d, (y + d) % NY).wait_send()
-    for step in range(half):
+    for way in range(2):
+        for piece in range(2):
+            for d in range(NH):
+                final(way, piece, d, head, (head + d) % NH).wait_send()
+    for step in range(half - 1):
         for piece in range(2):
             for way in range(2):
                 if step > 0 or piece == way:
@@ -701,8 +770,11 @@
             pltpu.VMEM((4, NH, BLOCK, HD), BF),
             pltpu.VMEM((2, QB, BLOCK, HD), F32),
             pltpu.VMEM((2, QB, BLOCK, HD), F32),
+            pltpu.VMEM((3, 2, NH, BLOCK, HD), BF),
             dma((4, NH - 1)),
             dma((4, NH - 1)),
+            dma((2, 2, NH)),
+            dma((2, 2, NH)),
             dma((2, NZ // 2, 2)),
             dma((2, NZ // 2, 2)),
             dma((NY - 1,)),
@@ -741,8 +813,8 @@
     kv, qg, wst = gather(*(pltpu.with_memory_space_constraint(r, pltpu.HBM) for r in rows))
     ids = pltpu.with_memory_space_constraint(random_ids.T, pltpu.HBM)
     global_ids = pltpu.with_memory_space_constraint(global_ids, pltpu.HBM)
-    st, pair_list = stats(ids, global_ids, kv, qg, wst)
-    dkv, row_stats = terms(pair_list, global_ids, share(st), kv, qg)
+    st, pair_list, *pairs = stats(ids, global_ids, kv, qg, wst)
+    dkv, row_stats = terms(pair_list, global_ids, share(st), kv, qg, pairs)
     return deliver(reduce(ids, global_ids, kv, qg, row_stats, dkv))
 
 

time: 143 us -> 131 us (0.916)
  Pallas kernels: 142 us -> 130 us
    pallas_call x1, Pallas kernels: 6.58 us -> 2.48 us  [terms(): pl.pallas_call(terms_kernel, out_shape=(jax.ShapeDtypeStruct((NZ, 2, QB,...]
    pallas_call x1, Pallas kernels: 61.1 us -> 57.4 us  [reduce(): pl.pallas_call(reduce_kernel, out_shape=(out,) * 4, in_specs=[smem()] * 2...]
    pallas_call x1, Pallas kernels: 64 us -> 60.7 us  [gather(): pl.pallas_call(gather_kernel, out_shape=(jax.ShapeDtypeStruct((NZ, 2, QB,...]
where the time goes in v4:
time: 131 us
  Pallas kernels  130 us (99%)
    pallas_call x1, Pallas kernels, gather(): pl.pallas_call(gather_kernel, out_shape=(jax.ShapeDtypeStruct((NZ, 2, QB,...  60.7 us
    pallas_call x1, Pallas kernels, reduce(): pl.pallas_call(reduce_kernel, out_shape=(out,) * 4, in_specs=[smem()] * 2...  57.4 us
    pallas_call x1, Pallas kernels, share(): pl.pallas_call(share_kernel, out_shape=jax.ShapeDtypeStruct((NY, 3, PLANE...  5.25 us
    pallas_call x1, Pallas kernels, stats(): pl.pallas_call(stats_kernel, out_shape=(jax.ShapeDtypeStruct((3, PLANE //...  3.11 us

profile of v4, /device:TPU:1, one launch (start us, length us, event | category | flops | bytes accessed | tf_op | source)
XLA Modules:
  0.0 130.6 jit_solution(16490825962820660312)
XLA Ops:
  0.6 60.7 %gather_rows.1 = (bf16[16,2,8,64,128]{4,3,2,1,0:T(8,128)(2,1)S(1)}, bf16[4,2,8,64,128]{4,3,2,1,0:T(8,128)(2,1)S(1)}, f32[3,16,128]{2,1,0:T(8,128)S(1)}) custom-call(bf16[64,1024]{1,0:T(8,128)(2,1)} %q_ref.1, bf16[64,1024]{1,0:T(8,128)(2,1)} %k_ref.1, bf16[64,1024]{1,0:T(8,128)(2,1)} %v_ref.1, bf16[64,1024]{1,0:T(8,128)(2,1)} %g_ref.1), custom_call_target="tpu_custom_call" | custom-call | tf_op jit(solution)/shard_map/gather_rows/pallas_call | solution.py:237
  61.3 3.1 %pair_stats.1 = (f32[3,16,128]{2,1,0:T(8,128)S(1)}, s32[144]{0:T(256)S(1)}, f32[3,2,5,16,128]{4,3,2,1,0:T(8,128)S(1)}, f32[112,64,64]{2,1,0:T(8,128)S(1)}, f32[112,64,64]{2,1,0:T(8,128)S(1)}) custom-call(s32[3,512]{1,0:T(4,128)} %bitcast.1, s32[2]{0:T(128)} %gids.5, bf16[16,2,8,64,128]{4,3,2,1,0:T(8,128)(2,1)S(1)} %get-tuple-element.18.kv_ref, ...), custom_call_target="tpu_custom_call" | custom-call | tf_op jit(solution)/shard_map/pair_stats/pallas_call | solution.py:369
  64.4 5.3 %share_stats.1.all_ref = f32[4,3,16,128]{3,2,1,0:T(8,128)S(1)} custom-call(f32[3,16,128]{2,1,0:T(8,128)S(1)} %get-tuple-element.22.st_ref), custom_call_target="tpu_custom_call" | custom-call | tf_op jit(solution)/shard_map/share_stats/pallas_call | solution.py:408
  69.7 2.5 %pair_terms.1 = (bf16[16,2,8,64,128]{4,3,2,1,0:T(8,128)(2,1)S(1)}, f32[3,2,16,128]{3,2,1,0:T(8,128)S(1)}) custom-call(s32[144]{0:T(256)S(1)} %get-tuple-element.21.list_ref, s32[2]{0:T(128)} %gids.5, f32[4,3,16,128]{3,2,1,0:T(8,128)S(1)} %share_stats.1.all_ref, bf16[16,2,8,64,128]{4,3,2,1,0:T(8,128)(2,1)S(1)} %get-tuple-element.18.kv_ref, ...), custom_call_target="tpu_custom_call" | custom-call | tf_op jit(solution)/shard_map/pair_terms/pallas_call | solution.py:502
  72.2 57.4 %reduce_rows.1 = (bf16[64,1024]{1,0:T(8,128)(2,1)S(1)}, bf16[64,1024]{1,0:T(8,128)(2,1)S(1)}, bf16[64,1024]{1,0:T(8,128)(2,1)S(1)}, bf16[64,1024]{1,0:T(8,128)(2,1)S(1)}) custom-call(s32[3,512]{1,0:T(4,128)} %bitcast.2, s32[2]{0:T(128)} %gids.5, bf16[16,2,8,64,128]{4,3,2,1,0:T(8,128)(2,1)S(1)} %get-tuple-element.18.kv_ref, ...), custom_call_target="tpu_custom_call" | custom-call | tf_op jit(solution)/shard_map/reduce_rows/pallas_call | solution.py:761
  129.6 0.8 deliver_rows.1

commit v5 on v4

--- a/solution.py
+++ b/solution.py
@@ -49,10 +49,11 @@
     return seq, head, seq // NZ, seq % NZ
 
 
-def greet(peers):
+def greet(peers, meanwhile=lambda: None):
     barrier = pltpu.get_barrier_semaphore()
     for seq, head in peers:
         pl.semaphore_signal(barrier, inc=1, device_id=(seq, head), device_id_type=MESH)
+    meanwhile()
     pl.semaphore_wait(barrier, len(peers))
 
 
@@ -261,19 +262,16 @@
     )(q, k, v, g)
 
 
-def stats_kernel(
-    ids, gids, kv_ref, qg_ref, wst_ref, st_ref, list_ref, one, expo_ref, dprob_ref, full
-):
+def stats_kernel(ids_ref, kv_ref, qg_ref, list_ref, one, expo_ref, dprob_ref, ids, sem):
     y = lax.axis_index("seq") // NZ
     z = lax.axis_index("seq") % NZ
     base = y * COL
+    fetch = pltpu.make_async_copy(ids_ref, ids, sem)
+    fetch.start()
     one[0] = jnp.full((2, 5, PLANE // 2, HD), FLOOR, F32)
-    full[0] = jnp.full((3, PLANE // 2, HD), FLOOR, F32)
     for k in range(1, 3):
         one[k] = jnp.zeros((2, 5, PLANE // 2, HD), F32)
-        full[k] = jnp.zeros((3, PLANE // 2, HD), F32)
-    for k in range(3):
-        full[k, 2] = wst_ref[k]
+    fetch.wait()
 
     def note(count, i, slot, block):
         rel = block - base
@@ -326,11 +324,48 @@
 
     lax.fori_loop(0, rounds, pairs, 0)
 
-    for n in range(2):
-        rel = gids[n] - base
-
-        @pl.when((rel >= 0) & (rel < COL))
-        def _(n=n, rel=rel):
+
+def tile_rows(qg_ref, t):
+    at = slice((t % 2) * 4, (t % 2) * 4 + 4)
+    queries = qg_ref[t // 2, 0, at].reshape(4 * BLOCK, HD)
+    grads = qg_ref[t // 2, 1, at].reshape(4 * BLOCK, HD)
+    return queries, grads
+
+
+def stats(ids, kv, qg):
+    return pl.pallas_call(
+        stats_kernel,
+        out_shape=(
+            jax.ShapeDtypeStruct((LIST,), jnp.int32),
+            jax.ShapeDtypeStruct((3, 2, 5, PLANE // 2, HD), F32),
+            jax.ShapeDtypeStruct((PAIRS, BLOCK, BLOCK), F32),
+            jax.ShapeDtypeStruct((PAIRS, BLOCK, BLOCK), F32),
+        ),
+        in_specs=[hbm(), vmem(), vmem()],
+        out_specs=(smem(), vmem(), vmem(), vmem()),
+        scratch_shapes=[
+            pltpu.SMEM((3, NZ * NY * QB), jnp.int32),
+            pltpu.SemaphoreType.DMA,
+        ],
+        compiler_params=pltpu.CompilerParams(vmem_limit_bytes=24 * MIB),
+        name="pair_stats",
+    )(ids, kv, qg)
+
+
+def share_kernel(
+    gids_ref, wst_ref, one, kv_ref, qg_ref, all_ref, full, st, gids, sem, send, recv
+):
+    seq, head, y, z = place()
+    base = y * COL
+    fetch = pltpu.make_async_copy(gids_ref, gids, sem)
+    fetch.start()
+
+    def total():
+        fetch.wait()
+        for n in range(2):
+            rel = gids[n] - base
+            good = (rel >= 0) & (rel < COL)
+            rel = jnp.clip(rel, 0, COL - 1)
             keys = kv_ref[rel >> 3, 0, rel & 7]
             values = kv_ref[rel >> 3, 1, rel & 7]
             for t in range(TILES):
@@ -339,89 +374,87 @@
                 dprobs = lax.dot_general(values, grads, NT, preferred_element_type=F32)
                 top = jnp.max(scores, axis=0, keepdims=True)
                 expo = jnp.exp(scores - top)
-                total = jnp.sum(expo, axis=0, keepdims=True)
-                delta = jnp.sum(expo * dprobs, axis=0, keepdims=True)
-                for k, found in enumerate((top, total, delta)):
+                found = (
+                    jnp.where(good, top, FLOOR),
+                    jnp.where(good, jnp.sum(expo, axis=0, keepdims=True), 0.0),
+                    jnp.where(good, jnp.sum(expo * dprobs, axis=0, keepdims=True), 0.0),
+                )
+                for k in range(3):
                     for p in range(2):
-                        full[k, n, 2 * t + p : 2 * t + p + 1] = found[:, p * HD : (p + 1) * HD]
-
-    def parts(k):
-        even = one[k, 0, 0:4]
-        odd = pltpu.roll(one[k, 1, 0:4].reshape(2 * PLANE, HD), BLOCK, 1)
-        return jnp.concatenate([even, odd.reshape(4, PLANE // 2, HD), full[k]], axis=0)
-
-    tops = parts(0)
-    top = jnp.max(tops, axis=0)
-    factor = jnp.exp(tops - top[None])
-    st_ref[0] = top
-    st_ref[1] = jnp.sum(parts(1) * factor, axis=0)
-    st_ref[2] = jnp.sum(parts(2) * factor, axis=0)
-
-
-def tile_rows(qg_ref, t):
-    at = slice((t % 2) * 4, (t % 2) * 4 + 4)
-    queries = qg_ref[t // 2, 0, at].reshape(4 * BLOCK, HD)
-    grads = qg_ref[t // 2, 1, at].reshape(4 * BLOCK, HD)
-    return queries, grads
-
-
-def stats(ids, gids, kv, qg, wst):
-    return pl.pallas_call(
-        stats_kernel,
-        out_shape=(
-            jax.ShapeDtypeStruct((3, PLANE // 2, HD), F32),
-            jax.ShapeDtypeStruct((LIST,), jnp.int32),
-            jax.ShapeDtypeStruct((3, 2, 5, PLANE // 2, HD), F32),
-            jax.ShapeDtypeStruct((PAIRS, BLOCK, BLOCK), F32),
-            jax.ShapeDtypeStruct((PAIRS, BLOCK, BLOCK), F32),
-        ),
-        in_specs=[smem(), smem(), vmem(), vmem(), vmem()],
-        out_specs=(vmem(), smem(), vmem(), vmem(), vmem()),
-        scratch_shapes=[
-            pltpu.VMEM((3, 3, PLANE // 2, HD), F32),
-        ],
-        compiler_params=pltpu.CompilerParams(vmem_limit_bytes=24 * MIB),
-        name="pair_stats",
-    )(ids, gids, kv, qg, wst)
-
-
-def share_kernel(st_ref, all_ref, send, recv):
-    seq, head, y, z = place()
-    greet(row_peers(y, z, head))
+                        full[k, n, 2 * t + p : 2 * t + p + 1] = found[k][:, p * HD : (p + 1) * HD]
+
+        def parts(k):
+            even = one[k, 0, 0:4]
+            odd = pltpu.roll(one[k, 1, 0:4].reshape(2 * PLANE, HD), BLOCK, 1)
+            odd = odd.reshape(4, PLANE // 2, HD)
+            return jnp.concatenate([even, odd, full[k], wst_ref[k][None]], axis=0)
+
+        tops = parts(0)
+        top = jnp.max(tops, axis=0)
+        factor = jnp.exp(tops - top[None])
+        st[0] = top
+        st[1] = jnp.sum(parts(1) * factor, axis=0)
+        st[2] = jnp.sum(parts(2) * factor, axis=0)
+
+    greet(row_peers(y, z, head), total)
 
     def row(d, sender, target):
-        return rcopy(
-            st_ref, all_ref.at[sender], send.at[d - 1], recv.at[d - 1], target * NZ + z, head
-        )
+        return rcopy(st, all_ref.at[sender], send.at[d - 1], recv.at[d - 1], target * NZ + z, head)
 
     for d in range(1, NY):
         row(d, y, (y + d) % NY).start()
-    all_ref[y] = st_ref[...]
+    all_ref[y] = st[...]
     for d in range(1, NY):
         row(d, (y + NY - d) % NY, (y + d) % NY).wait_recv()
     for d in range(1, NY):
         row(d, y, (y + d) % NY).wait_send()
 
 
-def share(st):
+def share(gids, wst, one, kv, qg):
     dma = pltpu.SemaphoreType.DMA
     return pl.pallas_call(
         share_kernel,
         out_shape=jax.ShapeDtypeStruct((NY, 3, PLANE // 2, HD), F32),
-        in_specs=[vmem()],
+        in_specs=[hbm()] + [vmem()] * 4,
         out_specs=vmem(),
-        scratch_shapes=[dma((NY - 1,)), dma((NY - 1,))],
+        scratch_shapes=[
+            pltpu.VMEM((3, 2, PLANE // 2, HD), F32),
+            pltpu.VMEM((3, PLANE // 2, HD), F32),
+            pltpu.SMEM((2,), jnp.int32),
+            dma,
+            dma((NY - 1,)),
+            dma((NY - 1,)),
+        ],
         compiler_params=pltpu.CompilerParams(
             collective_id=1, has_side_effects=True, vmem_limit_bytes=8 * MIB
         ),
         name="share_stats",
-    )(st)
+    )(gids, wst, one, kv, qg)
 
 
 def terms_kernel(
-    list_ref, gids, all_ref, kv_ref, qg_ref, one, expo_ref, dprob_ref, dkv_ref, shifted, scale_ref
+    list_hbm,
+    gids_hbm,
+    all_ref,
+    kv_ref,
+    qg_ref,
+    one,
+    expo_ref,
+    dprob_ref,
+    dkv_ref,
+    shifted,
+    scale_ref,
+    list_ref,
+    gids,
+    fetched,
 ):
     base = (lax.axis_index("seq") // NZ) * COL
+    fetches = [
+        pltpu.make_async_copy(list_hbm, list_ref, fetched.at[0]),
+        pltpu.make_async_copy(gids_hbm, gids, fetched.at[1]),
+    ]
+    for fetch in fetches:
+        fetch.start()
     tops = all_ref[:, 0]
     top = jnp.max(tops, axis=0)
     factor = jnp.exp(tops - top[None])
@@ -441,6 +474,8 @@
         return carry
 
     lax.fori_loop(0, NZ, clear_kv, 0)
+    for fetch in fetches:
+        fetch.wait()
     rounds = list_ref[LIST - 1]
 
     def add_kv(rel, dk, dv):
@@ -505,17 +540,22 @@
             jax.ShapeDtypeStruct((NZ, 2, QB, BLOCK, HD), BF),
             jax.ShapeDtypeStruct((3, 2, PLANE // 2, HD), F32),
         ),
-        in_specs=[smem(), smem()] + [vmem()] * 6,
+        in_specs=[pl.BlockSpec(memory_space=pl.ANY), hbm()] + [vmem()] * 6,
         out_specs=(vmem(),) * 2,
-        scratch_shapes=[pltpu.VMEM((2, 5, PLANE // 2, HD), F32)],
+        scratch_shapes=[
+            pltpu.VMEM((2, 5, PLANE // 2, HD), F32),
+            pltpu.SMEM((LIST,), jnp.int32),
+            pltpu.SMEM((2,), jnp.int32),
+            pltpu.SemaphoreType.DMA((2,)),
+        ],
         compiler_params=pltpu.CompilerParams(vmem_limit_bytes=32 * MIB),
         name="pair_terms",
     )(pair_list, gids, all_stats, kv, qg, *pairs)
 
 
 def reduce_kernel(
-    ids,
-    gids,
+    ids_ref,
+    gids_ref,
     kv_ref,
     qg_ref,
     rows_ref,
@@ -531,6 +571,9 @@
     near_kv,
     near_oq,
     fin,
+    ids,
+    gids,
+    fetched,
     hs,
     hr,
     fs,
@@ -541,6 +584,12 @@
     yr,
 ):
     seq, head, y, z = place()
+    fetches = [
+        pltpu.make_async_copy(ids_ref, ids, fetched.at[0]),
+        pltpu.make_async_copy(gids_ref, gids, fetched.at[1]),
+    ]
+    for fetch in fetches:
+        fetch.start()
     greet(head_peers(seq, head) + near_planes(y, z) + row_peers(y, z, head))
     right = y * NZ + (z + 1) % NZ
     left = y * NZ + (z + NZ - 1) % NZ
@@ -696,6 +745,8 @@
     for way, piece in ((0, 1), (1, 0)):
         hop(way, 1, piece).start()
     near_kv[...] = jnp.zeros((2, QB, BLOCK, HD), F32)
+    for fetch in fetches:
+        fetch.wait()
     for n in range(0, 6, 2):
         far_some(n, 2)
 
@@ -761,7 +812,7 @@
     return pl.pallas_call(
         reduce_kernel,
         out_shape=(out,) * 4,
-        in_specs=[smem()] * 2 + [vmem()] * 4,
+        in_specs=[hbm()] * 2 + [vmem()] * 4,
         out_specs=(vmem(),) * 4,
         scratch_shapes=[
             pltpu.VMEM((2, NZ // 2, 2, QB, BLOCK, HD), BF),
@@ -771,6 +822,9 @@
             pltpu.VMEM((2, QB, BLOCK, HD), F32),
             pltpu.VMEM((2, QB, BLOCK, HD), F32),
             pltpu.VMEM((3, 2, NH, BLOCK, HD), BF),
+            pltpu.SMEM((3, NZ * NY * QB), jnp.int32),
+            pltpu.SMEM((2,), jnp.int32),
+            dma((2,)),
             dma((4, NH - 1)),
             dma((4, NH - 1)),
             dma((2, 2, NH)),
@@ -813,8 +867,9 @@
     kv, qg, wst = gather(*(pltpu.with_memory_space_constraint(r, pltpu.HBM) for r in rows))
     ids = pltpu.with_memory_space_constraint(random_ids.T, pltpu.HBM)
     global_ids = pltpu.with_memory_space_constraint(global_ids, pltpu.HBM)
-    st, pair_list, *pairs = stats(ids, global_ids, kv, qg, wst)
-    dkv, row_stats = terms(pair_list, global_ids, share(st), kv, qg, pairs)
+    pair_list, one, *pairs = stats(ids, kv, qg)
+    sums = share(global_ids, wst, one, kv, qg)
+    dkv, row_stats = terms(pair_list, global_ids, sums, kv, qg, (one, *pairs))
     return deliver(reduce(ids, global_ids, kv, qg, row_stats, dkv))
 
 

time: 131 us -> 129 us (0.985)
  Pallas kernels: 130 us -> 128 us
where the time goes in v5:
time: 129 us
  Pallas kernels  128 us (99%)
    pallas_call x1, Pallas kernels, gather(): pl.pallas_call(gather_kernel, out_shape=(jax.ShapeDtypeStruct((NZ, 2, QB,...  60.7 us
    pallas_call x1, Pallas kernels, reduce(): pl.pallas_call(reduce_kernel, out_shape=(out,) * 4, in_specs=[hbm()] * 2...  56.1 us
    pallas_call x1, Pallas kernels, share(): pl.pallas_call(share_kernel, out_shape=jax.ShapeDtypeStruct((NY, 3, PLANE...  5.41 us
    pallas_call x1, Pallas kernels, stats(): pl.pallas_call(stats_kernel, out_shape=(jax.ShapeDtypeStruct((LIST,), jnp...  3.08 us

profile of v5, /device:TPU:1, one launch (start us, length us, event | category | flops | bytes accessed | tf_op | source)
XLA Modules:
  0.0 128.8 jit_solution(10676198691699185892)
XLA Ops:
  0.6 60.7 %gather_rows.1 = (bf16[16,2,8,64,128]{4,3,2,1,0:T(8,128)(2,1)S(1)}, bf16[4,2,8,64,128]{4,3,2,1,0:T(8,128)(2,1)S(1)}, f32[3,16,128]{2,1,0:T(8,128)S(1)}) custom-call(bf16[64,1024]{1,0:T(8,128)(2,1)} %q_ref.1, bf16[64,1024]{1,0:T(8,128)(2,1)} %k_ref.1, bf16[64,1024]{1,0:T(8,128)(2,1)} %v_ref.1, bf16[64,1024]{1,0:T(8,128)(2,1)} %g_ref.1), custom_call_target="tpu_custom_call" | custom-call | tf_op jit(solution)/shard_map/gather_rows/pallas_call | solution.py:238
  61.3 3.1 %pair_stats.1 = (s32[144]{0:T(256)S(1)}, f32[3,2,5,16,128]{4,3,2,1,0:T(8,128)S(1)}, f32[112,64,64]{2,1,0:T(8,128)S(1)}, f32[112,64,64]{2,1,0:T(8,128)S(1)}) custom-call(s32[3,512]{1,0:T(4,128)} %bitcast.1, bf16[16,2,8,64,128]{4,3,2,1,0:T(8,128)(2,1)S(1)} %get-tuple-element.17.kv_ref, bf16[4,2,8,64,128]{4,3,2,1,0:T(8,128)(2,1)S(1)} %get-tuple-element.18.qg_ref), custom_call_target="tpu_custom_call" | custom-call | tf_op jit(solution)/shard_map/pair_stats/pallas_call | solution.py:336
  64.4 5.4 %share_stats.1.all_ref = f32[4,3,16,128]{3,2,1,0:T(8,128)S(1)} custom-call(s32[2]{0:T(128)} %gids_ref.3, f32[3,16,128]{2,1,0:T(8,128)S(1)} %get-tuple-element.20.wst_ref, f32[3,2,5,16,128]{4,3,2,1,0:T(8,128)S(1)} %get-tuple-element.21.one, bf16[16,2,8,64,128]{4,3,2,1,0:T(8,128)(2,1)S(1)} %get-tuple-element.17.kv_ref, ...), custom_call_target="tpu_custom_call" | custom-call | tf_op jit(solution)/shard_map/share_stats/pallas_call | solution.py:415
  69.8 1.9 %pair_terms.1 = (bf16[16,2,8,64,128]{4,3,2,1,0:T(8,128)(2,1)S(1)}, f32[3,2,16,128]{3,2,1,0:T(8,128)S(1)}) custom-call(s32[144]{0:T(256)S(1)} %get-tuple-element.19.list_hbm, s32[2]{0:T(128)} %gids_ref.3, f32[4,3,16,128]{3,2,1,0:T(8,128)S(1)} %share_stats.1.all_ref, bf16[16,2,8,64,128]{4,3,2,1,0:T(8,128)(2,1)S(1)} %get-tuple-element.17.kv_ref, ...), custom_call_target="tpu_custom_call" | custom-call | tf_op jit(solution)/shard_map/pair_terms/pallas_call | solution.py:537
  71.7 56.1 %reduce_rows.1 = (bf16[64,1024]{1,0:T(8,128)(2,1)S(1)}, bf16[64,1024]{1,0:T(8,128)(2,1)S(1)}, bf16[64,1024]{1,0:T(8,128)(2,1)S(1)}, bf16[64,1024]{1,0:T(8,128)(2,1)S(1)}) custom-call(s32[3,512]{1,0:T(4,128)} %bitcast.2, s32[2]{0:T(128)} %gids_ref.3, bf16[16,2,8,64,128]{4,3,2,1,0:T(8,128)(2,1)S(1)} %get-tuple-element.17.kv_ref, ...), custom_call_target="tpu_custom_call" | custom-call | tf_op jit(solution)/shard_map/reduce_rows/pallas_call | solution.py:812
  127.8 0.8 deliver_rows.1

commit v6 on v5

--- a/solution.py
+++ b/solution.py
@@ -689,7 +689,7 @@
             far(d, b)
             return carry
 
-        lax.fori_loop(start % QB, start % QB + count, one, 0, unroll=True)
+        lax.fori_loop(start % QB, start % QB + count, one, 0)
         if d < NY and start % QB + count == QB:
             row(d, (y + d) % NY).start()
 

time: 129 us -> 130 us (level)
  no operation moved by 1% of the time
where the time goes in v6:
time: 130 us; the launch traced here: 129 us
  Pallas kernels  129 us (99%)
    pallas_call x1, Pallas kernels, gather(): pl.pallas_call(gather_kernel, out_shape=(jax.ShapeDtypeStruct((NZ, 2, QB,...  60.7 us
    pallas_call x1, Pallas kernels, reduce(): pl.pallas_call(reduce_kernel, out_shape=(out,) * 4, in_specs=[hbm()] * 2...  57.3 us
    pallas_call x1, Pallas kernels, share(): pl.pallas_call(share_kernel, out_shape=jax.ShapeDtypeStruct((NY, 3, PLANE...  5.24 us
    pallas_call x1, Pallas kernels, stats(): pl.pallas_call(stats_kernel, out_shape=(jax.ShapeDtypeStruct((LIST,), jnp...  3.09 us

profile of v6, /device:TPU:1, one launch (start us, length us, event | category | flops | bytes accessed | tf_op | source)
XLA Modules:
  0.0 129.5 jit_solution(10433399403108419456)
XLA Ops:
  0.6 60.7 %gather_rows.1 = (bf16[16,2,8,64,128]{4,3,2,1,0:T(8,128)(2,1)S(1)}, bf16[4,2,8,64,128]{4,3,2,1,0:T(8,128)(2,1)S(1)}, f32[3,16,128]{2,1,0:T(8,128)S(1)}) custom-call(bf16[64,1024]{1,0:T(8,128)(2,1)} %q_ref.1, bf16[64,1024]{1,0:T(8,128)(2,1)} %k_ref.1, bf16[64,1024]{1,0:T(8,128)(2,1)} %v_ref.1, bf16[64,1024]{1,0:T(8,128)(2,1)} %g_ref.1), custom_call_target="tpu_custom_call" | custom-call | tf_op jit(solution)/shard_map/gather_rows/pallas_call | solution.py:238
  61.3 3.1 %pair_stats.1 = (s32[144]{0:T(256)S(1)}, f32[3,2,5,16,128]{4,3,2,1,0:T(8,128)S(1)}, f32[112,64,64]{2,1,0:T(8,128)S(1)}, f32[112,64,64]{2,1,0:T(8,128)S(1)}) custom-call(s32[3,512]{1,0:T(4,128)} %bitcast.1, bf16[16,2,8,64,128]{4,3,2,1,0:T(8,128)(2,1)S(1)} %get-tuple-element.17.kv_ref, bf16[4,2,8,64,128]{4,3,2,1,0:T(8,128)(2,1)S(1)} %get-tuple-element.18.qg_ref), custom_call_target="tpu_custom_call" | custom-call | tf_op jit(solution)/shard_map/pair_stats/pallas_call | solution.py:336
  64.4 5.2 %share_stats.1.all_ref = f32[4,3,16,128]{3,2,1,0:T(8,128)S(1)} custom-call(s32[2]{0:T(128)} %gids_ref.3, f32[3,16,128]{2,1,0:T(8,128)S(1)} %get-tuple-element.20.wst_ref, f32[3,2,5,16,128]{4,3,2,1,0:T(8,128)S(1)} %get-tuple-element.21.one, bf16[16,2,8,64,128]{4,3,2,1,0:T(8,128)(2,1)S(1)} %get-tuple-element.17.kv_ref, ...), custom_call_target="tpu_custom_call" | custom-call | tf_op jit(solution)/shard_map/share_stats/pallas_call | solution.py:415
  69.7 1.7 %pair_terms.1 = (bf16[16,2,8,64,128]{4,3,2,1,0:T(8,128)(2,1)S(1)}, f32[3,2,16,128]{3,2,1,0:T(8,128)S(1)}) custom-call(s32[144]{0:T(256)S(1)} %get-tuple-element.19.list_hbm, s32[2]{0:T(128)} %gids_ref.3, f32[4,3,16,128]{3,2,1,0:T(8,128)S(1)} %share_stats.1.all_ref, bf16[16,2,8,64,128]{4,3,2,1,0:T(8,128)(2,1)S(1)} %get-tuple-element.17.kv_ref, ...), custom_call_target="tpu_custom_call" | custom-call | tf_op jit(solution)/shard_map/pair_terms/pallas_call | solution.py:537
  71.3 57.3 %reduce_rows.1 = (bf16[64,1024]{1,0:T(8,128)(2,1)S(1)}, bf16[64,1024]{1,0:T(8,128)(2,1)S(1)}, bf16[64,1024]{1,0:T(8,128)(2,1)S(1)}, bf16[64,1024]{1,0:T(8,128)(2,1)S(1)}) custom-call(s32[3,512]{1,0:T(4,128)} %bitcast.2, s32[2]{0:T(128)} %gids_ref.3, bf16[16,2,8,64,128]{4,3,2,1,0:T(8,128)(2,1)S(1)} %get-tuple-element.17.kv_ref, ...), custom_call_target="tpu_custom_call" | custom-call | tf_op jit(solution)/shard_map/reduce_rows/pallas_call | solution.py:812
  128.7 0.8 deliver_rows.1

commit v7 on v5

--- a/solution.py
+++ b/solution.py
@@ -290,7 +290,7 @@
                 count = note(count, g * QB + b, r, ids[r, first + b])
             return count
 
-        count = lax.fori_loop(0, QB, scan, count, unroll=4)
+        count = lax.fori_loop(0, QB, scan, count, unroll=8)
     for u in range(UNROLL):
         list_ref[count + u] = jnp.int32(TRASH)
     rounds = (count + UNROLL - 1) >> 3
@@ -473,7 +473,7 @@
         dkv_ref[b] = jnp.zeros((2, QB, BLOCK, HD), BF)
         return carry
 
-    lax.fori_loop(0, NZ, clear_kv, 0)
+    lax.fori_loop(0, NZ, clear_kv, 0, unroll=4)
     for fetch in fetches:
         fetch.wait()
     rounds = list_ref[LIST - 1]

time: 129 us -> 130 us (level)
  no operation moved by 1% of the time
where the time goes in v7:
time: 130 us
  Pallas kernels  129 us (99%)
    pallas_call x1, Pallas kernels, gather(): pl.pallas_call(gather_kernel, out_shape=(jax.ShapeDtypeStruct((NZ, 2, QB,...  60.7 us
    pallas_call x1, Pallas kernels, reduce(): pl.pallas_call(reduce_kernel, out_shape=(out,) * 4, in_specs=[hbm()] * 2...  56.5 us
    pallas_call x1, Pallas kernels, share(): pl.pallas_call(share_kernel, out_shape=jax.ShapeDtypeStruct((NY, 3, PLANE...  5.71 us
    pallas_call x1, Pallas kernels, terms(): pl.pallas_call(terms_kernel, out_shape=(jax.ShapeDtypeStruct((NZ, 2, QB,...  3.01 us
    pallas_call x1, Pallas kernels, stats(): pl.pallas_call(stats_kernel, out_shape=(jax.ShapeDtypeStruct((LIST,), jnp...  2.71 us

profile of v7, /device:TPU:1, one launch (start us, length us, event | category | flops | bytes accessed | tf_op | source)
XLA Modules:
  0.0 130.2 jit_solution(11221922978361737267)
XLA Ops:
  0.6 60.7 %gather_rows.1 = (bf16[16,2,8,64,128]{4,3,2,1,0:T(8,128)(2,1)S(1)}, bf16[4,2,8,64,128]{4,3,2,1,0:T(8,128)(2,1)S(1)}, f32[3,16,128]{2,1,0:T(8,128)S(1)}) custom-call(bf16[64,1024]{1,0:T(8,128)(2,1)} %q_ref.1, bf16[64,1024]{1,0:T(8,128)(2,1)} %k_ref.1, bf16[64,1024]{1,0:T(8,128)(2,1)} %v_ref.1, bf16[64,1024]{1,0:T(8,128)(2,1)} %g_ref.1), custom_call_target="tpu_custom_call" | custom-call | tf_op jit(solution)/shard_map/gather_rows/pallas_call | solution.py:238
  61.3 2.7 %pair_stats.1 = (s32[144]{0:T(256)S(1)}, f32[3,2,5,16,128]{4,3,2,1,0:T(8,128)S(1)}, f32[112,64,64]{2,1,0:T(8,128)S(1)}, f32[112,64,64]{2,1,0:T(8,128)S(1)}) custom-call(s32[3,512]{1,0:T(4,128)} %bitcast.1, bf16[16,2,8,64,128]{4,3,2,1,0:T(8,128)(2,1)S(1)} %get-tuple-element.17.kv_ref, bf16[4,2,8,64,128]{4,3,2,1,0:T(8,128)(2,1)S(1)} %get-tuple-element.18.qg_ref), custom_call_target="tpu_custom_call" | custom-call | tf_op jit(solution)/shard_map/pair_stats/pallas_call | solution.py:336
  64.0 5.7 %share_stats.1.all_ref = f32[4,3,16,128]{3,2,1,0:T(8,128)S(1)} custom-call(s32[2]{0:T(128)} %gids_ref.3, f32[3,16,128]{2,1,0:T(8,128)S(1)} %get-tuple-element.20.wst_ref, f32[3,2,5,16,128]{4,3,2,1,0:T(8,128)S(1)} %get-tuple-element.21.one, bf16[16,2,8,64,128]{4,3,2,1,0:T(8,128)(2,1)S(1)} %get-tuple-element.17.kv_ref, ...), custom_call_target="tpu_custom_call" | custom-call | tf_op jit(solution)/shard_map/share_stats/pallas_call | solution.py:415
  69.8 3.0 %pair_terms.1 = (bf16[16,2,8,64,128]{4,3,2,1,0:T(8,128)(2,1)S(1)}, f32[3,2,16,128]{3,2,1,0:T(8,128)S(1)}) custom-call(s32[144]{0:T(256)S(1)} %get-tuple-element.19.list_hbm, s32[2]{0:T(128)} %gids_ref.3, f32[4,3,16,128]{3,2,1,0:T(8,128)S(1)} %share_stats.1.all_ref, bf16[16,2,8,64,128]{4,3,2,1,0:T(8,128)(2,1)S(1)} %get-tuple-element.17.kv_ref, ...), custom_call_target="tpu_custom_call" | custom-call | tf_op jit(solution)/shard_map/pair_terms/pallas_call | solution.py:537
  72.8 56.5 %reduce_rows.1 = (bf16[64,1024]{1,0:T(8,128)(2,1)S(1)}, bf16[64,1024]{1,0:T(8,128)(2,1)S(1)}, bf16[64,1024]{1,0:T(8,128)(2,1)S(1)}, bf16[64,1024]{1,0:T(8,128)(2,1)S(1)}) custom-call(s32[3,512]{1,0:T(4,128)} %bitcast.2, s32[2]{0:T(128)} %gids_ref.3, bf16[16,2,8,64,128]{4,3,2,1,0:T(8,128)(2,1)S(1)} %get-tuple-element.17.kv_ref, ...), custom_call_target="tpu_custom_call" | custom-call | tf_op jit(solution)/shard_map/reduce_rows/pallas_call | solution.py:812
  129.2 0.8 deliver_rows.1
